TPU v7x, 32 devices: a whole 2x2x4 slice. The times are simulated.
32 devices in a mesh: dp: 8 (over z, core), shard: 4 (over y, x).
Axes of the slice: x: 2, y: 2, z: 4, core: 2. Of those that a mesh axis runs over, the one named last changes fastest.
Arguments:
- tokens: bfloat16 [12288, 512], P(('dp', 'shard')), may hold values from -24 to 24
- w_proj: bfloat16 [512, 2048], P(None, 'shard'), may hold values from -0.25 to 0.25
- w_out: bfloat16 [512, 512], replicated, may hold values from -0.25 to 0.25
- item_rows: bfloat16 [4096, 512], P('shard'), may hold values from -1.5 to 1.5
- lengths: int32 [32, 4], P(('dp', 'shard')), may hold values from 1 to 192, 384 in all within a row
- target_owner: int32 [12288, 1], P(('dp', 'shard')), may hold values from 0 to 3; in each aligned block of 384 rows (0 to 383, 384 to 767, ...) at most 192 rows name the same one
- target_row: int32 [12288], P(('dp', 'shard')), may hold values from 0 to 1023
- negative_rows: int32 [256], P('shard'), may hold values from 0 to 1023
Outputs:
- grad_tokens: bfloat16 [12288, 512], P(('dp', 'shard'))
- weight_grads: float32 [512, 512], replicated
- item_grads: float32 [4096, 512], P('shard')
Inputs may be any that keep to these rules, and one draw needn't show every extreme that they name: `target_owner`: in the rows of one device no owner is named more than 192 times, a bound that some block reaches.
All inputs are finite; a program needn't handle non-finite values.
Results may differ from a plain program's by a relative error of at most 0.02.
Values may be sent and summed in bfloat16 or wider, within the bound.
A program may use at most 64 MiB of HBM per device.

v0:
```python
import jax
import jax.numpy as jnp
from jax import lax
from jax.sharding import PartitionSpec as P

D = 512
HEADS = 4
DH = 128
MAXLEN = 192


epsilon = 1e-06
logit_divisor = 0.015625
loss_scale = 512.0


def reduce_last_dimension(operand, other_side):
    return lax.dot_general(
        operand, other_side, (((1,), (1,)), ((), ())), preferred_element_type=jnp.float32
    )


def contract_first(operand, other_side):
    return lax.dot_general(
        operand, other_side, (((0,), (0,)), ((), ())), preferred_element_type=jnp.float32
    )


def silu_slope(values):
    sigmoid = jax.nn.sigmoid(values)
    return sigmoid * (1.0 + values * (1.0 - sigmoid))


def history_mask(lengths_row, rows_count):
    history_ends = jnp.cumsum(lengths_row)
    positions = jnp.arange(rows_count, dtype=jnp.int32)
    history_ids = jnp.sum((positions[:, None] >= history_ends[None, :-1]).astype(jnp.int32), axis=1)
    visible = (history_ids[:, None] == history_ids[None, :]) & (
        positions[None, :] <= positions[:, None]
    )
    return jnp.where(visible, 1.0, 0.0).astype(jnp.float32)


def head_columns(activated, section, head_index):
    first_col = section * D + head_index * DH
    return activated[:, first_col : first_col + DH]


def head_scores(queries, key_rows):
    return reduce_last_dimension(queries, key_rows) * DH ** (-0.5)


def head_weights(scores, visible):
    return (jax.nn.silu(scores) * visible * (1.0 / MAXLEN)).astype(jnp.bfloat16)


def forward_layer(tokens, project, w_out, visible):
    wide_tokens = tokens.astype(jnp.float32)
    input_scale = lax.rsqrt(jnp.mean(wide_tokens * wide_tokens, axis=1, keepdims=True) + epsilon)
    normed = (wide_tokens * input_scale).astype(jnp.bfloat16)
    pre_act = project(normed)
    activated = lax.optimization_barrier(jax.nn.silu(pre_act).astype(jnp.bfloat16))
    heads_out = []
    for head_index in range(HEADS):
        queries = head_columns(activated, 2, head_index)
        key_rows = head_columns(activated, 3, head_index)
        value_rows = head_columns(activated, 1, head_index)
        weights = head_weights(head_scores(queries, key_rows), visible)
        heads_out.append(jnp.dot(weights, value_rows, preferred_element_type=jnp.float32))
    joined = lax.optimization_barrier(jnp.concatenate(heads_out, axis=1).astype(jnp.bfloat16))
    joined_wide = joined.astype(jnp.float32)
    middle_scale = lax.rsqrt(jnp.mean(joined_wide * joined_wide, axis=1, keepdims=True) + epsilon)
    gate_wide = activated[:, :D].astype(jnp.float32)
    gated = (joined_wide * middle_scale * gate_wide).astype(jnp.bfloat16)
    layer_out = wide_tokens + jnp.dot(gated, w_out, preferred_element_type=jnp.float32)
    return (layer_out, (wide_tokens, input_scale, pre_act, activated, joined, middle_scale, gated))


def loss_head(layer_out, clicked_product_vectors, sampled_decoys):
    out_scale = lax.rsqrt(jnp.sum(layer_out * layer_out, axis=1, keepdims=True) + epsilon)
    normalized_example_vectors = lax.optimization_barrier(
        (layer_out * out_scale).astype(jnp.bfloat16)
    )
    normalized_complete_embedding = normalized_example_vectors.astype(jnp.float32)
    correct_logit_entry = (
        jnp.sum(normalized_complete_embedding * clicked_product_vectors.astype(jnp.float32), axis=1)
        / logit_divisor
    )
    decoy_logit_entries = (
        reduce_last_dimension(normalized_example_vectors, sampled_decoys) / logit_divisor
    )
    target_exp = jnp.exp(correct_logit_entry)
    negative_exp = jnp.exp(decoy_logit_entries)
    totals = target_exp + jnp.sum(negative_exp, axis=1)
    target_prob = target_exp / totals
    negative_probs = (loss_scale * negative_exp / totals[:, None]).astype(jnp.bfloat16)
    target_coef = (loss_scale * (target_prob - 1.0))[:, None]
    grad_unit = target_coef * clicked_product_vectors.astype(jnp.float32) + jnp.dot(
        negative_probs, sampled_decoys, preferred_element_type=jnp.float32
    )
    grad_out = out_scale * grad_unit - layer_out * out_scale**3 * jnp.sum(
        layer_out * grad_unit, axis=1, keepdims=True
    )
    grad_target = target_coef * normalized_complete_embedding
    return (grad_out, grad_target, negative_probs, normalized_example_vectors)


def backward_layer(grad_out, saved_state, project_back, w_out, visible):
    wide_tokens, input_scale, pre_act, activated, joined, middle_scale, gated = saved_state
    grad_out_b = grad_out.astype(jnp.bfloat16)
    weight_part = contract_first(gated, grad_out_b)
    grad_gated = reduce_last_dimension(grad_out_b, w_out)
    joined_wide = joined.astype(jnp.float32)
    gate_wide = activated[:, :D].astype(jnp.float32)
    grad_gate = grad_gated * joined_wide * middle_scale
    grad_norm = grad_gated * gate_wide
    grad_joined = middle_scale * grad_norm - joined_wide * middle_scale**3 * jnp.mean(
        joined_wide * grad_norm, axis=1, keepdims=True
    )
    grad_joined_b = grad_joined.astype(jnp.bfloat16)
    grad_values = []
    grad_queries = []
    grad_keys = []
    for head_index in range(HEADS):
        queries = head_columns(activated, 2, head_index)
        key_rows = head_columns(activated, 3, head_index)
        value_rows = head_columns(activated, 1, head_index)
        scores = head_scores(queries, key_rows)
        weights = head_weights(scores, visible)
        grad_head = grad_joined_b[:, head_index * DH : (head_index + 1) * DH]
        grad_weights = reduce_last_dimension(grad_head, value_rows)
        grad_values.append(contract_first(weights, grad_head))
        grad_scores = (
            grad_weights * visible * (1.0 / MAXLEN) * silu_slope(scores) * DH ** (-0.5)
        ).astype(jnp.bfloat16)
        grad_queries.append(jnp.dot(grad_scores, key_rows, preferred_element_type=jnp.float32))
        grad_keys.append(contract_first(grad_scores, queries))
    grad_act = jnp.concatenate([grad_gate] + grad_values + grad_queries + grad_keys, axis=1)
    grad_pre = (grad_act * silu_slope(pre_act)).astype(jnp.bfloat16)
    grad_normed = project_back(grad_pre)
    grad_input = input_scale * grad_normed - wide_tokens * input_scale**3 * jnp.mean(
        wide_tokens * grad_normed, axis=1, keepdims=True
    )
    return ((grad_out + grad_input).astype(jnp.bfloat16), weight_part)


def finish_rows(grad_items, rows_wide):
    item_scale = lax.rsqrt(jnp.sum(rows_wide * rows_wide, axis=1, keepdims=True) + epsilon)
    return (
        item_scale * grad_items
        - rows_wide * item_scale**3 * jnp.sum(rows_wide * grad_items, axis=1, keepdims=True)
    ) / loss_scale


def shards(tokens, w_proj, w_out, item_rows, lengths, target_owner, target_row, negative_rows):
    tok_rows = tokens.shape[0]
    model_width = tokens.shape[1]
    shard_count = lax.axis_size("shard")
    capacity = 2 * tok_rows // shard_count
    visible = history_mask(lengths[0], tok_rows)

    def project(normed):
        return jnp.dot(
            normed,
            lax.all_gather(w_proj, "shard", axis=1, tiled=True),
            preferred_element_type=jnp.float32,
        )

    def project_back(grad_pre):
        return reduce_last_dimension(grad_pre, lax.all_gather(w_proj, "shard", axis=1, tiled=True))

    rows_wide = item_rows.astype(jnp.float32)
    item_scale = lax.rsqrt(jnp.sum(rows_wide * rows_wide, axis=1, keepdims=True) + epsilon)
    unit_items = (rows_wide * item_scale).astype(jnp.bfloat16)
    owners = target_owner[:, 0]
    owner_hits = (owners[:, None] == jnp.arange(shard_count, dtype=jnp.int32)[None, :]).astype(
        jnp.int32
    )
    earlier = jnp.cumsum(owner_hits, axis=0) - owner_hits
    slot_index = jnp.sum(earlier * owner_hits, axis=1)
    position = owners * capacity + slot_index
    requests = jnp.zeros((shard_count * capacity,), jnp.int32).at[position].set(target_row)
    asked_rows = lax.all_to_all(
        requests.reshape(shard_count, capacity), "shard", split_axis=0, concat_axis=0, tiled=True
    )
    asked_flat = asked_rows.reshape(-1)
    served = jnp.take(unit_items, asked_flat, axis=0).reshape(shard_count, capacity, model_width)
    fetched = lax.all_to_all(served, "shard", split_axis=0, concat_axis=0, tiled=True)
    clicked_product_vectors = jnp.take(
        fetched.reshape(shard_count * capacity, model_width), position, axis=0
    )
    sampled_decoys = lax.all_gather(
        jnp.take(unit_items, negative_rows, axis=0), "shard", axis=0, tiled=True
    )
    layer_out, saved_state = forward_layer(tokens, project, w_out, visible)
    grad_out, grad_target, negative_probs, normalized_example_vectors = loss_head(
        layer_out, clicked_product_vectors, sampled_decoys
    )
    grad_tokens, weight_part = backward_layer(grad_out, saved_state, project_back, w_out, visible)
    outgoing = (
        jnp.zeros((shard_count * capacity, model_width), jnp.float32).at[position].set(grad_target)
    )
    returned = lax.all_to_all(
        outgoing.reshape(shard_count, capacity, model_width).astype(jnp.bfloat16),
        "shard",
        split_axis=0,
        concat_axis=0,
        tiled=True,
    ).astype(jnp.float32)
    grad_items = (
        jnp.zeros((item_rows.shape[0], model_width), jnp.float32)
        .at[asked_flat]
        .add(returned.reshape(-1, model_width))
    )
    own_negatives = lax.psum_scatter(
        contract_first(negative_probs, normalized_example_vectors).astype(jnp.bfloat16),
        "shard",
        scatter_dimension=0,
        tiled=True,
    ).astype(jnp.float32)
    grad_items = grad_items.at[negative_rows].add(own_negatives)
    share_rows = item_rows.shape[0] // lax.axis_size("dp")
    summed_share = lax.psum_scatter(
        grad_items.astype(jnp.bfloat16), "dp", scatter_dimension=0, tiled=True
    ).astype(jnp.float32)
    share_start = lax.axis_index("dp") * share_rows
    share_wide = lax.dynamic_slice_in_dim(rows_wide, share_start, share_rows, 0)
    item_grads = lax.all_gather(
        finish_rows(summed_share, share_wide).astype(jnp.bfloat16), "dp", axis=0, tiled=True
    ).astype(jnp.float32)
    weight_grads = lax.psum(weight_part, ("dp", "shard")) / loss_scale
    return (grad_tokens, weight_grads, item_grads)


def solution(mesh):
    in_specs = (
        P(("dp", "shard"), None),
        P(None, "shard"),
        P(),
        P("shard", None),
        P(("dp", "shard"), None),
        P(("dp", "shard"), None),
        P(("dp", "shard")),
        P("shard"),
    )
    out_specs = (P(("dp", "shard"), None), P(), P("shard", None))
    return jax.shard_map(shards, mesh=mesh, in_specs=in_specs, out_specs=out_specs, check_vma=False)
```

profile of v0, /device:TPU:9, one launch (start us, length us, event | category | flops | bytes accessed | tf_op | source)
XLA Modules:
  0.0 326.2 jit_solution(2457208400850158504)
XLA Ops:
  7.2 0.7 all-gather.3.cloned.1.call-update
  7.9 0.7 reduce
  8.6 1.2 reduce-window.11
  10.4 1.3 and_reduce_fusion
  11.7 3.1 scatter_custom_fusion
  14.8 0.7 all_to_all.12
  15.4 3.4 %all-to-all-start = ((s32[4,1,192]{2,1,0:T(1,128)}), s32[4,1,192]{2,1,0:T(1,128)S(1)}, u32[]{:S(2)}, u32[]{:S(2)}) async-start(s32[4,1,192]{2,1,0:T(1,128)} %all_to_all.12), calls=%async_computation | async-start | bytes 8192 | tf_op jit(solution)/shard_map/all_to_all | solution.py:183
  18.9 0.8 reduce-window.10
  19.7 1.2 fusion.24
  20.9 1.5 multiply_reduce_fusion
  22.4 0.7 compare_select_fusion.3
  23.0 0.7 compare_and_fusion.1
  24.0 0.7 convert_reduce_fusion
  24.7 1.7 convert_element_type.130
  26.5 2.7 gather_fusion
  29.2 1.1 broadcast_select_fusion
  30.3 3.6 %all-to-all-start.1 = ((bf16[4,192,512]{2,1,0:T(8,128)(2,1)}), bf16[4,192,512]{2,1,0:T(8,128)(2,1)S(1)}, u32[]{:S(2)}, u32[]{:S(2)}) async-start(bf16[4,192,512]{2,1,0:T(8,128)(2,1)} %broadcast_select_fusion), calls=%async_computation.1 | async-start | bytes 1572864 | tf_op jit(solution)/shard_map/all_to_all | solution.py:188
  33.9 0.6 multiply_multiply_fusion
  34.5 0.7 gather_fusion.2
  35.3 22.2 %all_gather.11 = bf16[256,512]{1,0:T(8,128)(2,1)S(1)} all-gather(bf16[64,512]{1,0:T(8,128)(2,1)S(1)} %broadcast_select_fusion.2), channel_id=1, replica_groups=mesh['dp'=8,'shard'=4] {'shard'}, dimensions={0}, use_global_device_ids=true | all-gather | bytes 327680 | tf_op jit(solution)/shard_map/all_gather | solution.py:192
  57.6 2.6 gather_fusion.1
  60.2 4.5 %multiply_convert_fusion.1 = (bf16[384,2048]{1,0:T(8,128)(2,1)S(1)}, f32[384,2048]{1,0:T(8,128)}) fusion(bf16[512,2048]{1,0:T(8,128)(2,1)} %all-gather.3.cloned.1.call-done, bf16[384,512]{1,0:T(8,128)(2,1)S(1)} %copy-done.8, f32[384]{0:T(512)S(1)} %get-tuple-element.12), kind=kOutput, calls=%fused_computation.8 | convolution fusion | flops 809828352 | bytes 7210496 | tf_op jit(solution)/shard_map/dot_general | solution.py:163
  65.5 1.6 fusion.40
  69.0 0.6 multiply_multiply_fusion.2
  70.4 0.6 fusion.101
  71.0 0.6 copy-done.34
  71.5 1.0 convolution_convert_fusion
  72.5 1.5 multiply_reduce_fusion.1
  74.1 1.4 multiply_subtract_fusion
  75.4 0.5 fusion.37
  76.3 0.6 copy-done.20
  77.8 1.7 copy-done.26
  79.5 1.1 fusion.18
  80.6 2.8 scatter_custom_fusion.1
  83.4 1.0 convert_element_type.142
  84.4 4.3 %all-to-all-start.2 = ((bf16[4,192,512]{2,1,0:T(8,128)(2,1)}), bf16[4,192,512]{2,1,0:T(8,128)(2,1)}, u32[]{:S(2)}, u32[]{:S(2)}) async-start(bf16[4,192,512]{2,1,0:T(8,128)(2,1)} %bitcast.58), calls=%async_computation.2 | async-start | bytes 1572864 | tf_op jit(solution)/shard_map/all_to_all | solution.py:203
  88.8 0.7 reduce-scatter.3.cloned.1.call-update
  89.7 2.0 convolution_dynamic-update-slice_fusion.8
  91.7 1.9 convolution_dynamic-update-slice_fusion.7
  93.6 2.2 fusion.17
  95.8 3.2 all-to-all-done.2
  99.1 8.9 %scatter_custom_fusion.2 = f32[1024,512]{1,0:T(8,128)} fusion(s32[768]{0:T(1024)S(1)} %fusion.98, bf16[768,512]{1,0:T(8,128)(2,1)} %bitcast.7, f32[]{:T(128)} %constant.51.clone.1), kind=kCustom, calls=%fused_computation.20 | custom fusion | flops 786432 | bytes 2883588 | tf_op jit(solution)/shard_map/scatter-add | solution.py:213
  108.0 10.7 %reduce-scatter.3.cloned.1.call-done = bf16[64,512]{1,0:T(8,128)(2,1)} async-done(((bf16[256,512]{1,0:T(8,128)(2,1)}), bf16[64,512]{1,0:T(8,128)(2,1)}) %reduce-scatter.3.cloned.1.call-update) | async-done | bytes 65552 | tf_op jit(solution)/shard_map/reduce_scatter | solution.py:215
  118.7 4.1 %scatter_custom_fusion.3 = f32[1024,512]{1,0:T(8,128)} fusion(f32[1024,512]{1,0:T(8,128)} %scatter_custom_fusion.2, s32[64]{0:T(128)} %copy-done.36, bf16[64,512]{1,0:T(8,128)(2,1)} %reduce-scatter.3.cloned.1.call-done), kind=kCustom, calls=%fused_computation.134 | custom fusion | flops 65536 | bytes 2162688 | tf_op jit(solution)/shard_map/scatter-add | solution.py:221
  122.8 2.7 convert_element_type.146
  125.6 1.9 convolution_dynamic-update-slice_fusion.6
  127.5 1.6 fusion.16
  129.1 0.9 convolution_dynamic-update-slice_fusion.5
  130.0 1.4 fusion.15
  131.4 0.9 convolution_dynamic-update-slice_fusion.4
  132.3 1.0 convolution_dynamic-update-slice_fusion.3
  133.4 1.0 convolution_dynamic-update-slice_fusion.2
  134.4 1.0 convolution_dynamic-update-slice_fusion.1
  135.3 1.5 fusion.56
  137.0 15.2 %reduce-scatter.5.cloned.1.call-done = bf16[128,512]{1,0:T(8,128)(2,1)} async-done(((bf16[1024,512]{1,0:T(8,128)(2,1)}), bf16[128,512]{1,0:T(8,128)(2,1)}) %reduce-scatter.5.cloned.1.call-update) | async-done | bytes 131088 | tf_op jit(solution)/shard_map/reduce_scatter | solution.py:223
  152.2 1.1 multiply_reduce_fusion.3
  153.3 1.8 fusion.54
  155.1 1.9 convolution_dynamic-update-slice_fusion
  157.1 4.9 %fusion.30 = (f32[384]{0:T(512)S(1)}, f32[384,512]{1,0:T(8,128)S(1)}) fusion(bf16[384,512]{1,0:T(8,128)(2,1)S(1)} %copy-done.10, bf16[512,2048]{1,0:T(8,128)(2,1)} %all-gather.3.cloned.1.call-done, f32[384,2048]{1,0:T(8,128)} %convolution_dynamic-update-slice_fusion, f32[384,2048]{1,0:T(8,128)} %get-tuple-element.24), kind=kOutput, calls=%fused_computation.88 | convolution fusion | flops 812973696 | bytes 9569792 | tf_op jit(solution)/shard_map/dot_general | solution.py:18
  162.0 1.0 fusion.29
  163.0 128.2 %all-reduce.2.cloned.1.call-done = f32[512,512]{1,0:T(8,128)} async-done(((f32[512,512]{1,0:T(8,128)}), f32[512,512]{1,0:T(8,128)}) %all-reduce.2.cloned.1.call-update) | async-done | bytes 1048592 | tf_op jit(solution)/shard_map/psum | solution.py:231
  291.2 2.3 broadcast_multiply_fusion
  293.5 23.4 %all-gather.5.cloned.1.call-done = bf16[1024,512]{1,0:T(8,128)(2,1)} async-done(((bf16[128,512]{1,0:T(8,128)(2,1)}), bf16[1024,512]{1,0:T(8,128)(2,1)}) %all-gather.5.cloned.1.call-update) | async-done | bytes 1048592 | tf_op jit(solution)/shard_map/all_gather | solution.py:228
  316.9 2.8 convert_element_type.149
  (121 shorter events, 6.1 us)
Async XLA Ops:
  7.2 61.2 %copy-start = (bf16[512,512]{1,0:T(8,128)(2,1)S(1)}, bf16[512,512]{1,0:T(8,128)(2,1)}, u32[]{:S(2)}) copy-start(bf16[512,512]{1,0:T(8,128)(2,1)} %param.10) | copy-start | bytes 1572868
  7.2 16.5 %copy-start.1 = (bf16[1024,512]{1,0:T(8,128)(2,1)S(1)}, bf16[1024,512]{1,0:T(8,128)(2,1)}, u32[]{:S(2)}) copy-start(bf16[1024,512]{1,0:T(8,128)(2,1)} %param.11) | copy-start | bytes 3145732
  7.2 53.0 %all-gather.3.cloned.1.call-start = ((), (), s32[]{:S(2)}) async-start(), calls=%async_computation.5 | async-start | bytes 2621440 | tf_op jit(solution)/shard_map/all_gather | solution.py:165
  11.7 22.2 %copy-start.28 = (s32[384]{0:T(512)}, s32[384]{0:T(512)S(1)}, u32[]{:S(2)}) copy-start(s32[384]{0:T(512)S(1)} %reduce.4) | copy-start | bytes 4612
  15.4 10.9 %all-to-all-start = ((s32[4,1,192]{2,1,0:T(1,128)}), s32[4,1,192]{2,1,0:T(1,128)S(1)}, u32[]{:S(2)}, u32[]{:S(2)}) async-start(s32[4,1,192]{2,1,0:T(1,128)} %all_to_all.12), calls=%async_computation | async-start | bytes 8192 | tf_op jit(solution)/shard_map/all_to_all | solution.py:183
  23.0 3.5 %copy-start.36 = (s32[64]{0:T(128)}, s32[64]{0:T(128)S(1)}, u32[]{:S(2)}) copy-start(s32[64]{0:T(128)S(1)} %compare_select_fusion.3) | copy-start | bytes 772
  30.3 27.3 %all-to-all-start.1 = ((bf16[4,192,512]{2,1,0:T(8,128)(2,1)}), bf16[4,192,512]{2,1,0:T(8,128)(2,1)S(1)}, u32[]{:S(2)}, u32[]{:S(2)}) async-start(bf16[4,192,512]{2,1,0:T(8,128)(2,1)} %broadcast_select_fusion), calls=%async_computation.1 | async-start | bytes 1572864 | tf_op jit(solution)/shard_map/all_to_all | solution.py:188
  34.5 25.6 %copy-start.30 = (f32[384]{0:T(512)}, f32[384]{0:T(512)S(1)}, u32[]{:S(2)}) copy-start(f32[384]{0:T(512)S(1)} %get-tuple-element.12) | copy-start | bytes 4612
  35.2 24.9 %copy-start.8 = (bf16[384,512]{1,0:T(8,128)(2,1)S(1)}, bf16[384,512]{1,0:T(8,128)(2,1)}, u32[]{:S(2)}) copy-start(bf16[384,512]{1,0:T(8,128)(2,1)} %param.8) | copy-start | bytes 1179652
  64.6 13.2 %copy-start.3 = (bf16[384,2048]{1,0:T(8,128)(2,1)}, bf16[384,2048]{1,0:T(8,128)(2,1)S(1)}, u32[]{:S(2)}) copy-start(bf16[384,2048]{1,0:T(8,128)(2,1)S(1)} %get-tuple-element.23) | copy-start | bytes 4718596
  64.6 0.8 copy-start.32
  64.9 2.2 copy-start.21
  65.2 1.9 copy-start.23
  65.5 1.6 copy-start.24
  67.1 1.3 copy-start.14
  67.1 1.3 copy-start.15
  67.1 1.8 copy-start.17
  67.1 1.8 copy-start.19
  67.1 1.3 copy-start.9
  68.4 1.6 copy-start.7
  68.4 1.6 copy-start.35
  68.9 3.6 %copy-start.5 = (f32[384,512]{1,0:T(8,128)}, f32[384,512]{1,0:T(8,128)S(1)}, u32[]{:S(2)}) copy-start(f32[384,512]{1,0:T(8,128)S(1)} %get-tuple-element.27) | copy-start | bytes 2359300
  69.7 1.3 copy-start.2
  70.0 0.9 copy-start.25
  71.0 0.6 copy-start.34
  76.0 1.0 copy-start.20
  76.0 1.2 copy-start.18
  76.0 1.5 copy-start.16
  76.0 3.5 %copy-start.33 = (s32[384]{0:T(512)S(1)}, s32[384]{0:T(512)}, u32[]{:S(2)}) copy-start(s32[384]{0:T(512)} %convert_reduce_fusion) | copy-start | bytes 4612
  76.0 3.5 %copy-start.37 = (f32[384,384]{1,0:T(8,128)S(1)}, f32[384,384]{1,0:T(8,128)}, u32[]{:S(2)}) copy-start(f32[384,384]{1,0:T(8,128)} %get-tuple-element.25) | copy-start | bytes 1769476
  76.3 1.5 copy-start.6
  77.8 1.7 copy-start.26
  79.5 1.1 copy-start.27
  84.4 7.3 %copy-start.4 = (bf16[384,2048]{1,0:T(8,128)(2,1)S(1)}, bf16[384,2048]{1,0:T(8,128)(2,1)}, u32[]{:S(2)}) copy-start(bf16[384,2048]{1,0:T(8,128)(2,1)} %copy-done.3) | copy-start | bytes 4718596
  84.4 14.7 %all-to-all-start.2 = ((bf16[4,192,512]{2,1,0:T(8,128)(2,1)}), bf16[4,192,512]{2,1,0:T(8,128)(2,1)}, u32[]{:S(2)}, u32[]{:S(2)}) async-start(bf16[4,192,512]{2,1,0:T(8,128)(2,1)} %bitcast.58), calls=%async_computation.2 | async-start | bytes 1572864 | tf_op jit(solution)/shard_map/all_to_all | solution.py:203
  88.7 29.9 %reduce-scatter.3.cloned.1.call-start = ((), (), s32[]{:S(2)}) async-start(), calls=%async_computation.7 | async-start | bytes 327680 | tf_op jit(solution)/shard_map/reduce_scatter | solution.py:215
  89.5 62.7 %reduce-scatter.5.cloned.1.call-start = ((), (), s32[]{:S(2)}) async-start(), calls=%async_computation.8 | async-start | bytes 1179648 | tf_op jit(solution)/shard_map/reduce_scatter | solution.py:223
  125.5 165.6 %all-reduce.2.cloned.1.call-start = ((), (), s32[]{:S(2)}) async-start(), calls=%async_computation.6 | async-start | bytes 2097152 | tf_op jit(solution)/shard_map/psum | solution.py:231
  127.5 2.5 copy-start.22
  130.0 2.3 copy-start.11
  130.0 3.4 %copy-start.13 = (bf16[384,384]{1,0:T(8,128)(2,1)S(1)}, bf16[384,384]{1,0:T(8,128)(2,1)}, u32[]{:S(2)}) copy-start(bf16[384,384]{1,0:T(8,128)(2,1)} %fusion.17) | copy-start | bytes 884740
  131.4 2.0 copy-start.12
  136.9 20.2 %copy-start.10 = (bf16[384,512]{1,0:T(8,128)(2,1)S(1)}, bf16[384,512]{1,0:T(8,128)(2,1)}, u32[]{:S(2)}) copy-start(bf16[384,512]{1,0:T(8,128)(2,1)} %param.8) | copy-start | bytes 1179652
  136.9 180.0 %all-gather.5.cloned.1.call-start = ((), (), s32[]{:S(2)}) async-start(), calls=%async_computation.9 | async-start | bytes 1179648 | tf_op jit(solution)/shard_map/all_gather | solution.py:228
  157.1 4.9 %copy-start.29 = (f32[384]{0:T(512)S(1)}, f32[384]{0:T(512)}, u32[]{:S(2)}) copy-start(f32[384]{0:T(512)} %get-tuple-element.11) | copy-start | bytes 4612
  157.1 4.9 %copy-start.31 = (f32[384]{0:T(512)S(1)}, f32[384]{0:T(512)}, u32[]{:S(2)}) copy-start(f32[384]{0:T(512)} %copy-done.30) | copy-start | bytes 4612
Sparse Core Ops, SparseCore 0:
  9.8 45.4 all-gather.2
  92.3 26.2 reduce-scatter.2
  125.7 26.4 reduce-scatter.4
  158.6 132.5 all-reduce.1
  293.2 23.6 all-gather.4
where the time goes:
time: 328 us; the launch traced here: 326 us
  waiting for transfers between devices  182 us (55%)
  other arithmetic  44.8 us (14%)
  matrix products  37.9 us (12%)
  blocking collectives  22.2 us (7%)
  between operations  14.3 us (4%)
  local copies, waits for them, and re-layouts  13.1 us (4%)
  starting transfers between devices  11.8 us (4%)
    psum x1, waiting for transfers between devices, shards(): weight_grads = lax.psum(weight_part, ('dp', 'shard')) / loss_scale  128 us
    all_gather x1, waiting for transfers between devices, shards(): lax.all_gather(finish_rows(summed_share, share_wide).astype(jnp.bfloat16)...  23.4 us
    all_gather x1, blocking collectives, shards(): lax.all_gather(jnp.take(unit_items, negative_rows, axis=0), 'shard', axis...  22.2 us
    reduce_scatter x1, waiting for transfers between devices, shards(): lax.psum_scatter(grad_items.astype(jnp.bfloat16), 'dp', scatter_dimension...  15.2 us
    dot_general x11, matrix products, reduce_last_dimension(): lax.dot_general(operand, other_side, (((1,), (1,)), ((), ())), preferred_...  14.5 us
    reduce_scatter x1, waiting for transfers between devices, shards(): lax.psum_scatter(contract_first(negative_probs, normalized_example_vector...  10.7 us
    dot_general x10, matrix products, contract_first(): lax.dot_general(operand, other_side, (((0,), (0,)), ((), ())), preferred_...  10.2 us
    scatter-add x1, other arithmetic, shards(): grad_items = jnp.zeros((item_rows.shape[0], model_width), jnp.float32).at...  8.93 us
  transfers between devices with their start and end apart: 8, of which 5 were waited for; matrix products, arithmetic and copies ran while one was open for 19% of the time, Pallas kernels for 0%

commit v1 on v0

--- a/solution.py
+++ b/solution.py
@@ -1,6 +1,10 @@
+import functools
+
 import jax
 import jax.numpy as jnp
 from jax import lax
+from jax.experimental import pallas as pl
+from jax.experimental.pallas import tpu as pltpu
 from jax.sharding import PartitionSpec as P
 
 D = 512
@@ -152,7 +156,7 @@
     ) / loss_scale
 
 
-def shards(tokens, w_proj, w_out, item_rows, lengths, target_owner, target_row, negative_rows):
+def plain_shards(tokens, w_proj, w_out, item_rows, lengths, target_owner, target_row, negative_rows):
     tok_rows = tokens.shape[0]
     model_width = tokens.shape[1]
     shard_count = lax.axis_size("shard")
@@ -232,6 +236,420 @@
     return (grad_tokens, weight_grads, item_grads)
 
 
+MESH = pl.DeviceIdType.MESH
+
+
+def start_copy(src, dst, sems, index, target):
+    send_sem, recv_sem = sems
+    copy = pltpu.make_async_remote_copy(
+        src_ref=src,
+        dst_ref=dst,
+        send_sem=send_sem.at[index],
+        recv_sem=recv_sem.at[index],
+        device_id=target,
+        device_id_type=MESH,
+    )
+    copy.start()
+    return copy
+
+
+def greet(peers):
+    barrier = pltpu.get_barrier_semaphore()
+    for peer in peers:
+        pl.semaphore_signal(barrier, inc=1, device_id=peer, device_id_type=MESH)
+    pl.semaphore_wait(barrier, len(peers))
+
+
+def places(n_dp, n_shard):
+    dp = lax.axis_index("dp")
+    shard = lax.axis_index("shard")
+    core = lax.rem(dp, 2)
+    height = dp // 2
+    sibling = (dp + 1 - 2 * core, shard)
+    shard_peers = [(dp, lax.rem(shard + k, n_shard)) for k in range(1, n_shard)]
+    shard_from = [lax.rem(shard + n_shard - k, n_shard) for k in range(1, n_shard)]
+    n_z = n_dp // 2
+    z_to = [lax.rem(height + k, n_z) for k in range(1, n_z)]
+    z_peers = [(z * 2 + core, shard) for z in z_to]
+    z_from = [lax.rem(height + n_z - k, n_z) for k in range(1, n_z)]
+    return dp, shard, core, height, sibling, shard_peers, shard_from, z_to, z_peers, z_from
+
+
+def token_slots(position, slots):
+    tok_rows = position.shape[0]
+    columns = lax.broadcasted_iota(jnp.int32, (tok_rows, slots), 1)
+    return columns == position
+
+
+def row_picks(asked_row, rows_count):
+    rows = lax.broadcasted_iota(jnp.int32, (rows_count, asked_row.shape[1]), 0)
+    return jnp.where(rows == asked_row, 1.0, 0.0).astype(jnp.bfloat16)
+
+
+def fetch_kernel(
+    n_dp,
+    n_shard,
+    capacity,
+    w_ref,
+    items_ref,
+    owner_col_ref,
+    owner_row_ref,
+    target_col_ref,
+    negative_col_ref,
+    w_full,
+    clicked,
+    negatives,
+    asked,
+    position_ref,
+    requests,
+    served,
+    fetched,
+    unit,
+    w_send,
+    w_recv,
+    pair_send,
+    pair_recv,
+    ask_send,
+    ask_recv,
+    neg_send,
+    neg_recv,
+    row_send,
+    row_recv,
+):
+    dp, shard, core, height, sibling, peers, sources, z_to, z_peers, z_from = places(n_dp, n_shard)
+    greet(peers + [sibling])
+    rows_count = items_ref.shape[0]
+    half = w_ref.shape[0] // 2
+    mine = pl.ds(pl.multiple_of(core * half, half), half)
+    copies = []
+    w_copies = []
+    for k, peer in enumerate(peers):
+        w_copies.append(
+            start_copy(w_ref.at[mine], w_full.at[shard, mine], (w_send, w_recv), k, peer)
+        )
+    owner_col = owner_col_ref[...]
+    tok_rows = owner_col.shape[0]
+    token_a = lax.broadcasted_iota(jnp.int32, (tok_rows, tok_rows), 0)
+    token_b = lax.broadcasted_iota(jnp.int32, (tok_rows, tok_rows), 1)
+    same = (owner_row_ref[...] == owner_col) & (token_b < token_a)
+    slot = jnp.sum(jnp.where(same, 1.0, 0.0), axis=1, keepdims=True).astype(jnp.int32)
+    position = owner_col * capacity + slot
+    position_ref[...] = position
+    slots = token_slots(position, n_shard * capacity)
+    target = target_col_ref[...].astype(jnp.float32)
+    request = jnp.sum(jnp.where(slots, target, 0.0), axis=0, keepdims=True).astype(jnp.int32)
+    for j in range(n_shard):
+        part = request[:, j * capacity : (j + 1) * capacity]
+        requests[j] = jnp.broadcast_to(part, (8, capacity))
+    ask_copies = []
+    for k, peer in enumerate(peers):
+        ask_copies.append(
+            start_copy(requests.at[peer[1]], asked.at[shard], (ask_send, ask_recv), k, peer)
+        )
+    asked[shard] = requests[shard]
+    rows_wide = items_ref[...].astype(jnp.float32)
+    item_scale = lax.rsqrt(jnp.sum(rows_wide * rows_wide, axis=1, keepdims=True) + epsilon)
+    unit[...] = (rows_wide * item_scale).astype(jnp.bfloat16)
+    neg_col = negative_col_ref[...]
+    neg_picks = token_slots(neg_col, rows_count)
+    negatives[shard] = jnp.dot(
+        jnp.where(neg_picks, 1.0, 0.0).astype(jnp.bfloat16),
+        unit[...],
+        preferred_element_type=jnp.float32,
+    ).astype(jnp.bfloat16)
+    neg_copies = []
+    for k, peer in enumerate(peers):
+        neg_copies.append(
+            start_copy(negatives.at[shard], negatives.at[shard], (neg_send, neg_recv), k, peer)
+        )
+    row_copies = []
+    for k, source in enumerate(sources):
+        ask_copies[k].wait_recv()
+        picks = row_picks(asked[source][0:1], rows_count)
+        served[source] = contract_first(picks, unit[...]).astype(jnp.bfloat16)
+        row_copies.append(
+            start_copy(
+                served.at[source], fetched.at[shard], (row_send, row_recv), k, (dp, source)
+            )
+        )
+    picks = row_picks(requests[shard][0:1], rows_count)
+    fetched[shard] = contract_first(picks, unit[...]).astype(jnp.bfloat16)
+    w_full[shard] = w_ref[...]
+    for k, source in enumerate(sources):
+        w_copies[k].wait_recv()
+        piece = w_full.at[source, mine]
+        copies.append(start_copy(piece, piece, (pair_send, pair_recv), k, sibling))
+    for copy in neg_copies + row_copies:
+        copy.wait_recv()
+    slots_one = jnp.where(slots, 1.0, 0.0).astype(jnp.bfloat16)
+    total = jnp.zeros(clicked.shape, jnp.float32)
+    for j in range(n_shard):
+        total += jnp.dot(
+            slots_one[:, j * capacity : (j + 1) * capacity],
+            fetched[j],
+            preferred_element_type=jnp.float32,
+        )
+    clicked[...] = total.astype(jnp.bfloat16)
+    for copy in copies:
+        copy.wait()
+    for copy in w_copies + ask_copies + neg_copies + row_copies:
+        copy.wait_send()
+
+
+def return_kernel(
+    n_dp,
+    n_shard,
+    capacity,
+    grad_target_ref,
+    neg_part_ref,
+    w_part_ref,
+    position_ref,
+    asked_ref,
+    negative_col_ref,
+    items_ref,
+    gathered,
+    w_gathered,
+    out_shard,
+    in_shard,
+    out_pair,
+    in_pair,
+    out_z,
+    in_z,
+    a_send,
+    a_recv,
+    b_send,
+    b_recv,
+    c_send,
+    c_recv,
+    d_send,
+    d_recv,
+    e_send,
+    e_recv,
+    f_send,
+    f_recv,
+    g_send,
+    g_recv,
+):
+    dp, shard, core, height, sibling, peers, sources, z_to, z_peers, z_from = places(n_dp, n_shard)
+    greet(peers + [sibling] + z_peers)
+    rows_count, width = items_ref.shape
+    n_z = n_dp // 2
+    neg_rows = negative_col_ref.shape[0]
+    w_rows = w_part_ref.shape[0] // n_shard
+    share = rows_count // n_dp
+    w_share = w_rows // n_dp
+    slots = token_slots(position_ref[...], n_shard * capacity)
+    slots_one = jnp.where(slots, 1.0, 0.0).astype(jnp.bfloat16)
+    grad_target = grad_target_ref[...]
+    for j in range(n_shard):
+        out_shard[j, 0:capacity] = contract_first(
+            slots_one[:, j * capacity : (j + 1) * capacity], grad_target
+        ).astype(jnp.bfloat16)
+        out_shard[j, capacity : capacity + neg_rows] = neg_part_ref[
+            j * neg_rows : (j + 1) * neg_rows
+        ].astype(jnp.bfloat16)
+        out_shard[j, capacity + neg_rows :] = w_part_ref[
+            j * w_rows : (j + 1) * w_rows
+        ].astype(jnp.bfloat16)
+    a_copies = []
+    for k, peer in enumerate(peers):
+        a_copies.append(
+            start_copy(out_shard.at[peer[1]], in_shard.at[shard], (a_send, a_recv), k, peer)
+        )
+    in_shard[shard] = out_shard[shard]
+    grad_items = jnp.zeros((rows_count, width), jnp.float32)
+    neg_sum = jnp.zeros((neg_rows, width), jnp.float32)
+    w_sum = jnp.zeros((w_rows, width), jnp.float32)
+    for source, copy in zip([shard] + sources, [None] + a_copies):
+        if copy is not None:
+            copy.wait_recv()
+        picks = row_picks(asked_ref[source][0:1], rows_count)
+        grad_items += jnp.dot(
+            picks, in_shard[source, 0:capacity], preferred_element_type=jnp.float32
+        )
+        neg_sum += in_shard[source, capacity : capacity + neg_rows].astype(jnp.float32)
+        w_sum += in_shard[source, capacity + neg_rows :].astype(jnp.float32)
+    neg_picks = token_slots(negative_col_ref[...], rows_count)
+    neg_ones = jnp.where(neg_picks, 1.0, 0.0).astype(jnp.bfloat16)
+    grad_items += contract_first(neg_ones, neg_sum.astype(jnp.bfloat16))
+    for z in range(n_z):
+        for c in range(2):
+            d = z * 2 + c
+            out_pair[c, z, 0:share] = grad_items[d * share : (d + 1) * share].astype(jnp.bfloat16)
+            out_pair[c, z, share:] = w_sum[d * w_share : (d + 1) * w_share].astype(jnp.bfloat16)
+    b_copy = start_copy(out_pair.at[1 - core], in_pair, (b_send, b_recv), 0, sibling)
+    b_copy.wait_recv()
+    out_z[...] = (
+        out_pair[core].astype(jnp.float32) + in_pair[...].astype(jnp.float32)
+    ).astype(jnp.bfloat16)
+    c_copies = []
+    for k, peer in enumerate(z_peers):
+        c_copies.append(
+            start_copy(out_z.at[z_to[k]], in_z.at[height], (c_send, c_recv), k, peer)
+        )
+    total = out_z[height].astype(jnp.float32)
+    for k, z in enumerate(z_from):
+        c_copies[k].wait_recv()
+        total += in_z[z].astype(jnp.float32)
+    own = pl.ds(pl.multiple_of(dp * share, share), share)
+    finished = finish_rows(total[0:share], items_ref[own].astype(jnp.float32))
+    gathered[core, height, 0:share] = finished.astype(jnp.bfloat16)
+    gathered[core, height, share:] = (total[share:] / loss_scale).astype(jnp.bfloat16)
+    d_copies = []
+    mine = gathered.at[core, height]
+    for k, peer in enumerate(z_peers):
+        d_copies.append(start_copy(mine, mine, (d_send, d_recv), k, peer))
+    e_copies = [start_copy(mine, mine, (e_send, e_recv), 0, sibling)]
+    for k, z in enumerate(z_from):
+        d_copies[k].wait_recv()
+        piece = gathered.at[core, z]
+        e_copies.append(start_copy(piece, piece, (e_send, e_recv), k + 1, sibling))
+    for z in range(n_z):
+        w_gathered[shard, core, z * w_share : (z + 1) * w_share] = gathered[core, z, share:]
+    f_copies = []
+    mine = w_gathered.at[shard, core]
+    for k, peer in enumerate(peers):
+        f_copies.append(start_copy(mine, mine, (f_send, f_recv), k, peer))
+    g_copies = [start_copy(mine, mine, (g_send, g_recv), 0, sibling)]
+    for k, source in enumerate(sources):
+        f_copies[k].wait_recv()
+        piece = w_gathered.at[source, core]
+        g_copies.append(start_copy(piece, piece, (g_send, g_recv), k + 1, sibling))
+    for copy in e_copies + g_copies:
+        copy.wait()
+    b_copy.wait_send()
+    for copy in a_copies + c_copies + d_copies + f_copies:
+        copy.wait_send()
+
+
+def dma(count):
+    return [pltpu.SemaphoreType.DMA((count,))] * 2
+
+
+def vmem_specs(count):
+    return [pl.BlockSpec(memory_space=pltpu.VMEM)] * count
+
+
+def shards(tokens, w_proj, w_out, item_rows, lengths, target_owner, target_row, negative_rows):
+    tok_rows, width = tokens.shape
+    n_shard = lax.axis_size("shard")
+    n_dp = lax.axis_size("dp")
+    n_z = n_dp // 2
+    capacity = 2 * tok_rows // n_shard
+    rows_count = item_rows.shape[0]
+    neg_rows = negative_rows.shape[0]
+    w_cols = w_proj.shape[1]
+    w_rows = width // n_shard
+    share = rows_count // n_dp
+    w_share = w_rows // n_dp
+    b16 = jnp.bfloat16
+    shape = jax.ShapeDtypeStruct
+    negative_col = negative_rows.reshape(-1, 1)
+    w_full, clicked, negatives, asked, position = pl.pallas_call(
+        functools.partial(fetch_kernel, n_dp, n_shard, capacity),
+        out_shape=[
+            shape((n_shard, width, w_cols), b16),
+            shape((tok_rows, width), b16),
+            shape((n_shard, neg_rows, width), b16),
+            shape((n_shard, 8, capacity), jnp.int32),
+            shape((tok_rows, 1), jnp.int32),
+        ],
+        in_specs=vmem_specs(6),
+        out_specs=vmem_specs(5),
+        scratch_shapes=[
+            pltpu.VMEM((n_shard, 8, capacity), jnp.int32),
+            pltpu.VMEM((n_shard, capacity, width), b16),
+            pltpu.VMEM((n_shard, capacity, width), b16),
+            pltpu.VMEM((rows_count, width), b16),
+        ]
+        + dma(n_shard - 1) * 5,
+        compiler_params=pltpu.CompilerParams(
+            collective_id=0, has_side_effects=True, vmem_limit_bytes=48 * 2**20
+        ),
+        name="fetch",
+    )(
+        w_proj,
+        item_rows,
+        target_owner,
+        target_owner.reshape(1, -1),
+        target_row.reshape(-1, 1),
+        negative_col,
+    )
+    visible = history_mask(lengths[0], tok_rows)
+
+    def project(normed):
+        return jnp.concatenate(
+            [
+                jnp.dot(normed, w_full[j], preferred_element_type=jnp.float32)
+                for j in range(n_shard)
+            ],
+            axis=1,
+        )
+
+    def project_back(grad_pre):
+        return sum(
+            reduce_last_dimension(grad_pre[:, j * w_cols : (j + 1) * w_cols], w_full[j])
+            for j in range(n_shard)
+        )
+
+    layer_out, saved_state = forward_layer(tokens, project, w_out, visible)
+    grad_out, grad_target, negative_probs, normalized = loss_head(
+        layer_out, clicked, negatives.reshape(-1, width)
+    )
+    grad_tokens, w_part = backward_layer(grad_out, saved_state, project_back, w_out, visible)
+    neg_part = contract_first(negative_probs, normalized)
+    gathered, w_gathered = pl.pallas_call(
+        functools.partial(return_kernel, n_dp, n_shard, capacity),
+        out_shape=[
+            shape((2, n_z, share + w_share, width), b16),
+            shape((n_shard, 2, n_z * w_share, width), b16),
+        ],
+        in_specs=vmem_specs(7),
+        out_specs=vmem_specs(2),
+        scratch_shapes=[
+            pltpu.VMEM((n_shard, capacity + neg_rows + w_rows, width), b16),
+            pltpu.VMEM((n_shard, capacity + neg_rows + w_rows, width), b16),
+            pltpu.VMEM((2, n_z, share + w_share, width), b16),
+            pltpu.VMEM((n_z, share + w_share, width), b16),
+            pltpu.VMEM((n_z, share + w_share, width), b16),
+            pltpu.VMEM((n_z, share + w_share, width), b16),
+        ]
+        + dma(n_shard - 1)
+        + dma(1)
+        + dma(n_z - 1) * 2
+        + dma(n_z)
+        + dma(n_shard - 1)
+        + dma(n_shard),
+        compiler_params=pltpu.CompilerParams(
+            collective_id=1, has_side_effects=True, vmem_limit_bytes=48 * 2**20
+        ),
+        name="give_back",
+    )(
+        grad_target.astype(b16),
+        neg_part.astype(b16),
+        w_part.astype(b16),
+        position,
+        asked,
+        negative_col,
+        item_rows,
+    )
+    item_grads = (
+        gathered[:, :, :share].transpose(1, 0, 2, 3).reshape(rows_count, width).astype(jnp.float32)
+    )
+    weight_grads = (
+        w_gathered.reshape(n_shard, 2, n_z, w_share, width)
+        .transpose(0, 2, 1, 3, 4)
+        .reshape(width, width)
+        .astype(jnp.float32)
+    )
+    return (grad_tokens, weight_grads, item_grads)
+
+
+def fits_kernels(mesh):
+    n_dp, n_shard = mesh.shape["dp"], mesh.shape["shard"]
+    return n_dp % 2 == 0 and n_dp > 2 and n_shard > 1 and D % (16 * n_dp * n_shard) == 0
+
+
 def solution(mesh):
     in_specs = (
         P(("dp", "shard"), None),
@@ -244,4 +662,6 @@
         P("shard"),
     )
     out_specs = (P(("dp", "shard"), None), P(), P("shard", None))
-    return jax.shard_map(shards, mesh=mesh, in_specs=in_specs, out_specs=out_specs, check_vma=False)
+    return jax.shard_map(
+        shards if fits_kernels(mesh) else plain_shards,
+        mesh=mesh, in_specs=in_specs, out_specs=out_specs, check_vma=False)

time: 328 us -> 115 us (0.35)
  waiting for transfers between devices: 182 us -> 0 us
  Pallas kernels: 0 us -> 84.6 us
  other arithmetic: 44.8 us -> 5.83 us
  matrix products: 37.9 us -> 13.6 us
  blocking collectives: 22.2 us -> 0 us
  between operations: 14.3 us -> 1.01 us
  starting transfers between devices: 11.8 us -> 0 us
  local copies, waits for them, and re-layouts: 13.1 us -> 8.22 us
    psum x1 -> x0, waiting for transfers between devices: 128 us -> none  [shards(): weight_grads = lax.psum(weight_part, ('dp', 'shard')) / loss_scale]
    pallas_call x0 -> x2, Pallas kernels: none -> 84.6 us  [the longest x1 57.9 us: shards(): pl.pallas_call(functools.partial(return_kernel, n_dp, n_shard, capacity),...]
    reduce_scatter x2 -> x0, waiting for transfers between devices: 25.9 us -> none  [the longest x1 15.2 us: shards(): lax.psum_scatter(grad_items.astype(jnp.bfloat16), 'dp', scatter_dimension...]
    all_gather x2 -> x0, waiting for transfers between devices: 23.4 us -> none  [the longest x1 23.4 us: shards(): lax.all_gather(finish_rows(summed_share, share_wide).astype(jnp.bfloat16)...]
    all_gather x1 -> x0, blocking collectives: 22.2 us -> none  [shards(): lax.all_gather(jnp.take(unit_items, negative_rows, axis=0), 'shard', axis...]
    scatter-add x2 -> x0, other arithmetic: 13.1 us -> none  [the longest x1 8.93 us: shards(): grad_items = jnp.zeros((item_rows.shape[0], model_width), jnp.float32).at...]
    all_to_all x3 -> x0, starting transfers between devices: 11.4 us -> none  [the longest x1 4.33 us: shards(): lax.all_to_all(outgoing.reshape(shard_count, capacity, model_width).astyp...]
    dot_general x11 -> x14, matrix products: 14.5 us -> 5.88 us  [reduce_last_dimension(): lax.dot_general(operand, other_side, (((1,), (1,)), ((), ())), preferred_...]
  transfers between devices with their start and end apart: 8 -> 0, of which waited for: 5 -> 0; matrix products, arithmetic and copies ran while one was open for 19% -> 0% of each run, Pallas kernels for 0% -> 0%
where the time goes in v1:
time: 115 us; the launch traced here: 113 us
  Pallas kernels  84.6 us (74%)
  matrix products  13.6 us (12%)
  local copies, waits for them, and re-layouts  8.22 us (7%)
  other arithmetic  5.83 us (5%)
    pallas_call x1, Pallas kernels, shards(): pl.pallas_call(functools.partial(return_kernel, n_dp, n_shard, capacity),...  57.9 us
    pallas_call x1, Pallas kernels, shards(): pl.pallas_call(functools.partial(fetch_kernel, n_dp, n_shard, capacity),...  26.7 us
    dot_general x14, matrix products, reduce_last_dimension(): lax.dot_general(operand, other_side, (((1,), (1,)), ((), ())), preferred_...  5.88 us
    unnamed x13, local copies, waits for them, and re-layouts  4.1 us
    dot_general x10, matrix products, contract_first(): lax.dot_general(operand, other_side, (((0,), (0,)), ((), ())), preferred_...  3.21 us

profile of v1, /device:TPU:9, one launch (start us, length us, event | category | flops | bytes accessed | tf_op | source)
XLA Modules:
  0.0 113.2 jit_solution(6219298861593041138)
XLA Ops:
  0.6 0.0 copy-start
  0.7 0.9 reduce-window.4
  1.6 0.1 convert_reduce_fusion
  1.7 0.8 copy.53.owner_col_ref
  2.5 0.8 reshape.108.target_col_ref
  3.3 0.7 copy.55.negative_col_ref
  4.0 1.2 %copy-done.1 = bf16[1024,512]{1,0:T(8,128)(2,1)S(1)} copy-done((bf16[1024,512]{1,0:T(8,128)(2,1)S(1)}, bf16[1024,512]{1,0:T(8,128)(2,1)}, u32[]{:S(2)}) %copy-start.1) | copy-done | bytes 1048600
  5.2 1.0 copy-done.3
  6.3 0.7 copy-done.4
  7.0 26.7 %fetch.1 = (bf16[4,512,512]{2,1,0:T(8,128)(2,1)S(1)}, bf16[384,512]{1,0:T(8,128)(2,1)S(1)}, bf16[4,64,512]{2,1,0:T(8,128)(2,1)S(1)}, s32[4,8,192]{2,1,0:T(8,128)S(1)}, s32[384,1]{1,0:T(8,128)S(1)}) custom-call(bf16[512,512]{1,0:T(8,128)(2,1)S(1)} %copy-done.3, bf16[1024,512]{1,0:T(8,128)(2,1)S(1)} %copy-done.1, s32[384,1]{1,0:T(8,128)S(1)} %copy.53.owner_col_ref, ...), custom_call_target="tpu_custom_call" | custom-call | tf_op jit(solution)/shard_map/fetch/pallas_call | solution.py:548
  33.6 0.2 fusion.20
  33.8 0.4 fusion.44
  34.2 0.4 fusion.47
  34.7 0.4 fusion.50
  35.1 0.4 fusion.54
  35.5 0.9 multiply_convert_fusion.1
  36.4 0.3 convolution_multiply_fusion
  36.7 0.3 convolution_multiply_fusion.1
  36.9 0.3 convolution_multiply_fusion.2
  37.2 0.9 fusion.35
  38.1 0.2 convolution_convert_fusion.2
  38.3 0.2 convolution_convert_fusion.3
  38.6 0.2 convolution_convert_fusion.4
  38.8 0.2 convolution_convert_fusion.5
  39.1 0.2 fusion.27
  39.3 0.5 multiply_reduce_fusion.1
  39.8 0.1 multiply_convert_fusion.2
  39.9 0.3 fusion.110
  40.3 0.2 fusion.19
  40.5 0.4 multiply_reduce_fusion
  40.9 0.2 multiply_subtract_fusion
  41.1 0.5 fusion.33
  41.7 0.3 fusion.32
  42.0 0.3 convolution_dynamic-update-slice_fusion.11
  42.3 0.3 convolution_dynamic-update-slice_fusion.10
  42.6 0.3 convolution_dynamic-update-slice_fusion.9
  42.8 0.3 convolution_dynamic-update-slice_fusion.8
  43.1 0.4 fusion.15
  43.5 0.2 convolution_dynamic-update-slice_fusion.7
  43.8 0.4 fusion.14
  44.2 0.2 convolution_dynamic-update-slice_fusion.6
  44.4 0.4 fusion.13
  44.9 0.2 convolution_dynamic-update-slice_fusion.5
  45.1 0.4 fusion.12
  45.5 0.2 convolution_dynamic-update-slice_fusion.4
  45.8 0.5 convolution_dynamic-update-slice_fusion.3
  46.2 0.3 convolution_dynamic-update-slice_fusion.2
  46.5 0.3 convolution_dynamic-update-slice_fusion.1
  46.8 0.3 convolution_dynamic-update-slice_fusion
  47.0 1.2 %multiply_convert_fusion = bf16[384,2048]{1,0:T(8,128)(2,1)S(1)} fusion(f32[384,2048]{1,0:T(8,128)S(1)} %convolution_dynamic-update-slice_fusion, f32[384,512]{1,0:T(8,128)S(1)} %fusion.44, f32[384,512]{1,0:T(8,128)S(1)} %fusion.47, f32[384,512]{1,0:T(8,128)S(1)} %fusion.50, f32[384,512]{1,0:T(8,128)S(1)} %fusion.54), kind=kLoop, calls=%fused_computation.1 | loop fusion | flops 9437184 | bytes 7864320 | tf_op jit(solution)/shard_map/convert_element_type | solution.py:143
  48.2 0.4 fusion.52
  48.6 0.4 convolution_add_fusion.2
  49.0 0.4 convolution_add_fusion.1
  49.4 0.5 fusion.26
  49.9 1.0 fusion.25
  51.0 0.1 fusion.18.grad_target_ref
  51.1 0.3 convolution_convert_fusion.1.neg_part_ref
  51.4 0.6 convolution_convert_fusion.w_part_ref
  52.0 0.3 copy-done.2
  52.3 57.9 %give_back.1 = (bf16[2,4,144,512]{3,2,1,0:T(8,128)(2,1)S(1)}, bf16[4,2,64,512]{3,2,1,0:T(8,128)(2,1)S(1)}) custom-call(bf16[384,512]{1,0:T(8,128)(2,1)S(1)} %fusion.18.grad_target_ref, bf16[256,512]{1,0:T(8,128)(2,1)S(1)} %convolution_convert_fusion.1.neg_part_ref, bf16[512,512]{1,0:T(8,128)(2,1)S(1)} %convolution_convert_fusion.w_part_ref, ...), custom_call_target="tpu_custom_call" | custom-call | tf_op jit(solution)/shard_map/give_back/pallas_call | solution.py:601
  110.2 0.1 convert_bitcast_fusion.1
  110.4 1.1 copy.73
  111.4 0.3 convert_bitcast_fusion
  111.7 1.5 %copy.74 = f32[4,2,128,512]{3,2,1,0:T(8,128)} copy(f32[4,2,128,512]{3,2,0,1:T(8,128)S(1)} %convert_bitcast_fusion) | data formatting | bytes 4194304 | tf_op jit(solution)/shard_map/convert_element_type | solution.py:637
  (15 shorter events, 0.1 us)
Async XLA Ops:
  0.6 38.6 %copy-start = (bf16[512,512]{1,0:T(8,128)(2,1)S(1)}, bf16[512,512]{1,0:T(8,128)(2,1)}, u32[]{:S(2)}) copy-start(bf16[512,512]{1,0:T(8,128)(2,1)} %param.10) | copy-start | bytes 1572868
  0.6 33.0 %copy-start.5 = (bf16[384,512]{1,0:T(8,128)(2,1)S(1)}, bf16[384,512]{1,0:T(8,128)(2,1)}, u32[]{:S(2)}) copy-start(bf16[384,512]{1,0:T(8,128)(2,1)} %param.8) | copy-start | bytes 1179652
  4.0 1.2 %copy-start.1 = (bf16[1024,512]{1,0:T(8,128)(2,1)S(1)}, bf16[1024,512]{1,0:T(8,128)(2,1)}, u32[]{:S(2)}) copy-start(bf16[1024,512]{1,0:T(8,128)(2,1)} %items_ref.3) | copy-start | bytes 3145732
  5.2 1.0 copy-start.3
  6.3 0.7 copy-start.4
  51.1 1.2 %copy-start.2 = (bf16[1024,512]{1,0:T(8,128)(2,1)S(1)}, bf16[1024,512]{1,0:T(8,128)(2,1)}, u32[]{:S(2)}) copy-start(bf16[1024,512]{1,0:T(8,128)(2,1)} %items_ref.3) | copy-start | bytes 3145732

commit v2 on v0

--- a/solution.py
+++ b/solution.py
@@ -1,6 +1,10 @@
+import functools
+
 import jax
 import jax.numpy as jnp
 from jax import lax
+from jax.experimental import pallas as pl
+from jax.experimental.pallas import tpu as pltpu
 from jax.sharding import PartitionSpec as P
 
 D = 512
@@ -152,7 +156,7 @@
     ) / loss_scale
 
 
-def shards(tokens, w_proj, w_out, item_rows, lengths, target_owner, target_row, negative_rows):
+def plain_shards(tokens, w_proj, w_out, item_rows, lengths, target_owner, target_row, negative_rows):
     tok_rows = tokens.shape[0]
     model_width = tokens.shape[1]
     shard_count = lax.axis_size("shard")
@@ -232,6 +236,518 @@
     return (grad_tokens, weight_grads, item_grads)
 
 
+MESH = pl.DeviceIdType.MESH
+
+
+def start_copy(src, dst, sems, index, target):
+    send_sem, recv_sem = sems
+    copy = pltpu.make_async_remote_copy(
+        src_ref=src,
+        dst_ref=dst,
+        send_sem=send_sem.at[index],
+        recv_sem=recv_sem.at[index],
+        device_id=target,
+        device_id_type=MESH,
+    )
+    copy.start()
+    return copy
+
+
+def places(n_dp, n_shard):
+    dp = lax.axis_index("dp")
+    shard = lax.axis_index("shard")
+    core = lax.rem(dp, 2)
+    height = dp // 2
+    sibling = (dp + 1 - 2 * core, shard)
+    shard_peers = [(dp, lax.rem(shard + k, n_shard)) for k in range(1, n_shard)]
+    shard_from = [lax.rem(shard + n_shard - k, n_shard) for k in range(1, n_shard)]
+    n_z = n_dp // 2
+    z_to = [lax.rem(height + k, n_z) for k in range(1, n_z)]
+    z_peers = [(z * 2 + core, shard) for z in z_to]
+    z_from = [lax.rem(height + n_z - k, n_z) for k in range(1, n_z)]
+    return dp, shard, core, height, sibling, shard_peers, shard_from, z_to, z_peers, z_from
+
+
+def one_hot_columns(position, slots):
+    columns = lax.broadcasted_iota(jnp.int32, (position.shape[0], slots), 1)
+    return columns == position
+
+
+def row_picks(asked_row, rows_count):
+    rows = lax.broadcasted_iota(jnp.int32, (rows_count, asked_row.shape[1]), 0)
+    return jnp.where(rows == asked_row, 1.0, 0.0).astype(jnp.bfloat16)
+
+
+def as_column(row):
+    count = row.shape[1]
+    across = lax.broadcasted_iota(jnp.int32, (count, count), 0)
+    along = lax.broadcasted_iota(jnp.int32, (count, count), 1)
+    return jnp.sum(jnp.where(across == along, row, 0), axis=1, keepdims=True)
+
+
+def as_row(column):
+    count = column.shape[0]
+    across = lax.broadcasted_iota(jnp.int32, (count, count), 0)
+    along = lax.broadcasted_iota(jnp.int32, (count, count), 1)
+    return jnp.sum(jnp.where(across == along, column, 0), axis=0, keepdims=True)
+
+
+def ones_of(picks):
+    return jnp.where(picks, 1.0, 0.0).astype(jnp.bfloat16)
+
+
+def visible_pairs(lengths, rows_count):
+    across = lax.broadcasted_iota(jnp.int32, (rows_count, rows_count), 0)
+    along = lax.broadcasted_iota(jnp.int32, (rows_count, rows_count), 1)
+    history_a = jnp.zeros((rows_count, rows_count), jnp.int32)
+    history_b = jnp.zeros((rows_count, rows_count), jnp.int32)
+    end = jnp.zeros((1, 1), jnp.int32)
+    for j in range(lengths.shape[1] - 1):
+        end = end + lengths[:, j : j + 1]
+        history_a += jnp.where(across >= end, 1, 0)
+        history_b += jnp.where(along >= end, 1, 0)
+    return jnp.where((history_a == history_b) & (along <= across), 1.0 / MAXLEN, 0.0)
+
+
+def layer_kernel(
+    n_dp,
+    n_shard,
+    capacity,
+    tokens_ref,
+    w_ref,
+    w_out_ref,
+    items_ref,
+    lengths_ref,
+    owner_ref,
+    target_ref,
+    negative_ref,
+    grad_tokens_ref,
+    gathered,
+    w_gathered,
+    w_full,
+    negatives,
+    requests,
+    asked,
+    served,
+    fetched,
+    unit,
+    pre,
+    act,
+    scores_ref,
+    visible_ref,
+    normed_ref,
+    joined_ref,
+    grad_joined_ref,
+    grad_out_ref,
+    grad_pre,
+    out_rows,
+    in_rows,
+    pair_sums,
+    pair_in,
+    out_sums,
+    in_sums,
+    out_pair,
+    in_pair,
+    out_z,
+    in_z,
+    send_sem,
+    recv_sem,
+):
+    dp, shard, core, height, sibling, peers, sources, z_to, z_peers, z_from = places(n_dp, n_shard)
+    n_z = n_dp // 2
+    others = sources
+    near = range(n_shard - 1)
+    barrier = pltpu.get_barrier_semaphore()
+    greeted = peers + [sibling] + z_peers
+    for peer in greeted:
+        pl.semaphore_signal(barrier, inc=1, device_id=peer, device_id_type=MESH)
+    used = [0]
+    started = []
+
+    def send(src, dst, target):
+        copy = start_copy(src, dst, (send_sem, recv_sem), used[0], target)
+        used[0] += 1
+        started.append(copy)
+        return copy
+
+    rows_count, width = items_ref.shape
+    tok_rows = tokens_ref.shape[0]
+    neg_rows = negative_ref.shape[1]
+    neg_half = neg_rows // 2
+    half = w_ref.shape[0] // 2
+    share = rows_count // n_dp
+    w_rows = width // n_shard
+    w_half = w_rows // 2
+    w_share = w_half // n_z
+    n_parts, part_cols = out_rows.shape[0], out_rows.shape[-1]
+
+    owner_col = owner_ref[...]
+    token_a = lax.broadcasted_iota(jnp.int32, (tok_rows, tok_rows), 0)
+    token_b = lax.broadcasted_iota(jnp.int32, (tok_rows, tok_rows), 1)
+    same = (as_row(owner_col) == owner_col) & (token_b < token_a)
+    slot = jnp.sum(jnp.where(same, 1.0, 0.0), axis=1, keepdims=True).astype(jnp.int32)
+    position = owner_col * capacity + slot
+    slots = one_hot_columns(position, n_shard * capacity)
+    target = as_column(target_ref[...])
+    request = jnp.sum(jnp.where(slots, target, 0), axis=0, keepdims=True)
+    for j in range(n_shard):
+        part = request[:, j * capacity : (j + 1) * capacity]
+        requests[j] = jnp.broadcast_to(part, (8, capacity))
+    slots_one = ones_of(slots)
+
+    pl.semaphore_wait(barrier, len(greeted))
+    ask_copies = [send(requests.at[peer[1]], asked.at[shard], peer) for peer in peers]
+    mine = pl.ds(pl.multiple_of(core * half, half), half)
+    w_copies = [send(w_ref.at[mine], w_full.at[shard, mine], peer) for peer in peers]
+    asked[shard] = requests[shard]
+
+    rows_wide = items_ref[...].astype(jnp.float32)
+    item_scale = lax.rsqrt(jnp.sum(rows_wide * rows_wide, axis=1, keepdims=True) + epsilon)
+    unit[...] = (rows_wide * item_scale).astype(jnp.bfloat16)
+    negative_col = as_column(negative_ref[...])
+    own_negatives = jnp.dot(
+        ones_of(one_hot_columns(negative_col, rows_count)),
+        unit[...],
+        preferred_element_type=jnp.float32,
+    ).astype(jnp.bfloat16)
+    negatives[shard, 0] = own_negatives[:neg_half]
+    negatives[shard, 1] = own_negatives[neg_half:]
+    neg_piece = negatives.at[shard, core]
+    neg_copies = [send(neg_piece, neg_piece, peer) for peer in peers]
+    w_full[shard] = w_ref[...]
+    wide_tokens = tokens_ref[...].astype(jnp.float32)
+    input_scale = lax.rsqrt(jnp.mean(wide_tokens * wide_tokens, axis=1, keepdims=True) + epsilon)
+    normed_ref[...] = (wide_tokens * input_scale).astype(jnp.bfloat16)
+    visible_ref[...] = visible_pairs(lengths_ref[...], tok_rows)
+
+    def section(j):
+        values = jnp.dot(normed_ref[...], w_full[j], preferred_element_type=jnp.float32)
+        pre[j] = values
+        act[j] = (values * lax.logistic(values)).astype(jnp.bfloat16)
+
+    section(shard)
+    for k, source in enumerate(others):
+        ask_copies[k].wait_recv()
+        picks = row_picks(asked[source][0:1], rows_count)
+        served[source] = contract_first(picks, unit[...]).astype(jnp.bfloat16)
+    picks = row_picks(requests[shard][0:1], rows_count)
+    fetched[shard] = contract_first(picks, unit[...]).astype(jnp.bfloat16)
+    w_pairs = []
+    for k, source in enumerate(others):
+        w_copies[k].wait_recv()
+        piece = w_full.at[source, mine]
+        w_pairs.append(send(piece, piece, sibling))
+    row_copies = [
+        send(served.at[source], fetched.at[shard], (dp, source)) for source in others
+    ]
+    neg_pairs = []
+    for k, source in enumerate(others):
+        neg_copies[k].wait_recv()
+        piece = negatives.at[source, core]
+        neg_pairs.append(send(piece, piece, sibling))
+    for k, source in enumerate(others):
+        w_pairs[k].wait_recv()
+        section(source)
+
+    def head_part(j, head):
+        return act[j, :, head * DH : (head + 1) * DH]
+
+    for head in range(HEADS):
+        scores = head_scores(head_part(2, head), head_part(3, head))
+        scores_ref[head] = scores
+        weights = (scores * lax.logistic(scores) * visible_ref[...]).astype(jnp.bfloat16)
+        joined_ref[:, head * DH : (head + 1) * DH] = jnp.dot(
+            weights, head_part(1, head), preferred_element_type=jnp.float32
+        ).astype(jnp.bfloat16)
+    joined_wide = joined_ref[...].astype(jnp.float32)
+    middle_scale = lax.rsqrt(jnp.mean(joined_wide * joined_wide, axis=1, keepdims=True) + epsilon)
+    gate_wide = act[0].astype(jnp.float32)
+    gated = (joined_wide * middle_scale * gate_wide).astype(jnp.bfloat16)
+    layer_out = tokens_ref[...].astype(jnp.float32) + jnp.dot(
+        gated, w_out_ref[...], preferred_element_type=jnp.float32
+    )
+    out_scale = lax.rsqrt(jnp.sum(layer_out * layer_out, axis=1, keepdims=True) + epsilon)
+    unit_b = (layer_out * out_scale).astype(jnp.bfloat16)
+    for copy in neg_pairs:
+        copy.wait_recv()
+    negative_exps = []
+    for j in range(n_shard):
+        for c in range(2):
+            logits = reduce_last_dimension(unit_b, negatives[j, c]) / logit_divisor
+            negative_exps.append(jnp.exp(logits))
+    negative_exp = jnp.concatenate(negative_exps, axis=1)
+    for copy in row_copies:
+        copy.wait_recv()
+    clicked = jnp.zeros((tok_rows, width), jnp.float32)
+    for j in range(n_shard):
+        clicked += jnp.dot(
+            slots_one[:, j * capacity : (j + 1) * capacity],
+            fetched[j],
+            preferred_element_type=jnp.float32,
+        )
+    unit_wide = unit_b.astype(jnp.float32)
+    target_logit = jnp.sum(unit_wide * clicked, axis=1, keepdims=True) / logit_divisor
+    target_exp = jnp.exp(target_logit)
+    totals = target_exp + jnp.sum(negative_exp, axis=1, keepdims=True)
+    negative_probs = (loss_scale * negative_exp / totals).astype(jnp.bfloat16)
+    target_coef = loss_scale * (target_exp / totals - 1.0)
+    grad_target = (target_coef * unit_wide).astype(jnp.bfloat16)
+
+    row_sends = []
+    for h in range(n_parts):
+        for j in range(n_shard):
+            out_rows[h, j] = contract_first(
+                slots_one[:, j * capacity : (j + 1) * capacity],
+                grad_target[:, h * part_cols : (h + 1) * part_cols],
+            ).astype(jnp.bfloat16)
+        if h == 0:
+            row_sends.append(
+                [send(out_rows.at[h, peer[1]], in_rows.at[h, shard], peer) for peer in peers]
+            )
+    grad_unit = target_coef * clicked
+    for j in range(n_shard):
+        for c in range(2):
+            first = (2 * j + c) * neg_half
+            grad_unit += jnp.dot(
+                negative_probs[:, first : first + neg_half],
+                negatives[j, c],
+                preferred_element_type=jnp.float32,
+            )
+    grad_out = out_scale * grad_unit - layer_out * out_scale**3 * jnp.sum(
+        layer_out * grad_unit, axis=1, keepdims=True
+    )
+    grad_out_ref[...] = grad_out
+    grad_out_b = grad_out.astype(jnp.bfloat16)
+    neg_part = contract_first(negative_probs, unit_b).astype(jnp.bfloat16)
+    w_part = contract_first(gated, grad_out_b).astype(jnp.bfloat16)
+    for h in range(n_parts):
+        cols = slice(h * part_cols, (h + 1) * part_cols)
+        for j in range(n_shard):
+            for c in range(2):
+                first = (2 * j + c) * neg_half
+                pair_sums[c, h, j, 0:neg_half] = neg_part[first : first + neg_half, cols]
+                first = (2 * j + c) * w_half
+                pair_sums[c, h, j, neg_half:] = w_part[first : first + w_half, cols]
+    sum_pair = send(pair_sums.at[1 - core], pair_in, sibling)
+    sum_pair.wait_recv()
+    out_sums[...] = (
+        pair_sums[core].astype(jnp.float32) + pair_in[...].astype(jnp.float32)
+    ).astype(jnp.bfloat16)
+    sum_sends = []
+    for h in range(n_parts):
+        if h > 0:
+            row_sends.append(
+                [send(out_rows.at[h, peer[1]], in_rows.at[h, shard], peer) for peer in peers]
+            )
+        sum_sends.append(
+            [send(out_sums.at[h, peer[1]], in_sums.at[h, shard], peer) for peer in peers]
+        )
+
+    grad_gated = reduce_last_dimension(grad_out_b, w_out_ref[...])
+    grad_pre[0] = (grad_gated * joined_wide * middle_scale * silu_slope(pre[0])).astype(
+        jnp.bfloat16
+    )
+    grad_norm = grad_gated * gate_wide
+    grad_joined_ref[...] = (
+        middle_scale * grad_norm
+        - joined_wide
+        * middle_scale**3
+        * jnp.mean(joined_wide * grad_norm, axis=1, keepdims=True)
+    ).astype(jnp.bfloat16)
+
+    def head_back(head):
+        cols = slice(head * DH, (head + 1) * DH)
+        scores = scores_ref[head]
+        sigmoid = lax.logistic(scores)
+        visible = visible_ref[...]
+        weights = (scores * sigmoid * visible).astype(jnp.bfloat16)
+        grad_head = grad_joined_ref[:, cols]
+        grad_weights = reduce_last_dimension(grad_head, head_part(1, head))
+        slope = sigmoid * (1.0 + scores * (1.0 - sigmoid))
+        grad_scores = (grad_weights * visible * slope * DH ** (-0.5)).astype(jnp.bfloat16)
+        grads = (
+            contract_first(weights, grad_head),
+            jnp.dot(grad_scores, head_part(3, head), preferred_element_type=jnp.float32),
+            contract_first(grad_scores, head_part(2, head)),
+        )
+        for j, grad in enumerate(grads):
+            grad_pre[j + 1, :, cols] = (grad * silu_slope(pre[j + 1, :, cols])).astype(
+                jnp.bfloat16
+            )
+
+    def collect(h):
+        grad_items = jnp.zeros((rows_count, part_cols), jnp.float32)
+        sums = jnp.zeros((neg_half + w_half, part_cols), jnp.float32)
+        for k, source in enumerate([shard] + others):
+            if k > 0:
+                row_sends[h][k - 1].wait_recv()
+                sum_sends[h][k - 1].wait_recv()
+            rows = out_rows[h, shard] if k == 0 else in_rows[h, source]
+            part = out_sums[h, shard] if k == 0 else in_sums[h, source]
+            picks = row_picks(asked[source][0:1], rows_count)
+            grad_items += jnp.dot(picks, rows, preferred_element_type=jnp.float32)
+            sums += part.astype(jnp.float32)
+        rows = lax.broadcasted_iota(jnp.int32, (neg_half, rows_count), 1)
+        own_rows = jnp.where(core == 0, negative_col[:neg_half], negative_col[neg_half:])
+        grad_items += contract_first(
+            ones_of(rows == own_rows), sums[0:neg_half].astype(jnp.bfloat16)
+        )
+        for z in range(n_z):
+            for c in range(2):
+                d = z * 2 + c
+                out_pair[h, c, z] = grad_items[d * share : (d + 1) * share].astype(jnp.bfloat16)
+            first = neg_half + z * w_share
+            out_z[h, z, share:] = sums[first : first + w_share].astype(jnp.bfloat16)
+        return send(out_pair.at[h, 1 - core], in_pair.at[h], sibling)
+
+    def pass_on(h, pair):
+        pair.wait_recv()
+        for z in range(n_z):
+            out_z[h, z, 0:share] = (
+                out_pair[h, core, z].astype(jnp.float32) + in_pair[h, z].astype(jnp.float32)
+            ).astype(jnp.bfloat16)
+        return [
+            send(out_z.at[h, z_to[k]], in_z.at[h, height], peer) for k, peer in enumerate(z_peers)
+        ]
+
+    head_back(0)
+    pair = collect(0)
+    head_back(1)
+    z_sends = [pass_on(0, pair)]
+    for h in range(1, n_parts):
+        pair = collect(h)
+        head_back(2)
+        z_sends.append(pass_on(h, pair))
+    for head in range(3 if n_parts > 1 else 2, HEADS):
+        head_back(head)
+    grad_normed = jnp.zeros((tok_rows, width), jnp.float32)
+    for j in range(n_shard):
+        grad_normed += reduce_last_dimension(grad_pre[j], w_full[j])
+    wide_tokens = tokens_ref[...].astype(jnp.float32)
+    grad_input = input_scale * grad_normed - wide_tokens * input_scale**3 * jnp.mean(
+        wide_tokens * grad_normed, axis=1, keepdims=True
+    )
+    grad_tokens_ref[...] = (grad_out_ref[...] + grad_input).astype(jnp.bfloat16)
+
+    totals_parts = []
+    for h in range(n_parts):
+        total = out_z[h, height].astype(jnp.float32)
+        for k, z in enumerate(z_from):
+            z_sends[h][k].wait_recv()
+            total += in_z[h, z].astype(jnp.float32)
+        totals_parts.append(total)
+    total = jnp.concatenate(totals_parts, axis=1)
+    w_gathered[shard, core, height] = (total[share:] / loss_scale).astype(jnp.bfloat16)
+    w_mine = w_gathered.at[shard, core, height]
+    w_z = [send(w_mine, w_mine, peer) for peer in z_peers]
+    own = pl.ds(pl.multiple_of(dp * share, share), share)
+    finished = finish_rows(total[0:share], items_ref[own].astype(jnp.float32))
+    gathered[core, height] = finished.astype(jnp.bfloat16)
+    items_mine = gathered.at[core, height]
+    items_z = [send(items_mine, items_mine, peer) for peer in z_peers]
+    last = [send(items_mine, items_mine, sibling)]
+    for copy in w_z:
+        copy.wait_recv()
+    w_block = w_gathered.at[shard, core]
+    w_around = [send(w_block, w_block, peer) for peer in peers]
+    last.append(send(w_block, w_block, sibling))
+    for k, source in enumerate(others):
+        w_around[k].wait_recv()
+        piece = w_gathered.at[source, core]
+        last.append(send(piece, piece, sibling))
+    for k, z in enumerate(z_from):
+        items_z[k].wait_recv()
+        piece = gathered.at[core, z]
+        last.append(send(piece, piece, sibling))
+    for copy in last:
+        copy.wait_recv()
+    for copy in started:
+        copy.wait_send()
+
+
+def vmem_specs(count):
+    return [pl.BlockSpec(memory_space=pltpu.VMEM)] * count
+
+
+def shards(tokens, w_proj, w_out, item_rows, lengths, target_owner, target_row, negative_rows):
+    tok_rows, width = tokens.shape
+    n_shard = lax.axis_size("shard")
+    n_dp = lax.axis_size("dp")
+    n_z = n_dp // 2
+    capacity = 2 * tok_rows // n_shard
+    rows_count = item_rows.shape[0]
+    neg_half = negative_rows.shape[0] // 2
+    share = rows_count // n_dp
+    w_half = width // n_shard // 2
+    w_share = w_half // n_z
+    parts = 2
+    cols = width // parts
+    b16 = jnp.bfloat16
+    f32 = jnp.float32
+    shape = jax.ShapeDtypeStruct
+    copies = 7 * (n_shard - 1) + 4 * parts * (n_shard + n_z) + 2 * (n_shard + n_z) + 8
+    grad_tokens, gathered, w_gathered = pl.pallas_call(
+        functools.partial(layer_kernel, n_dp, n_shard, capacity),
+        out_shape=[
+            shape((tok_rows, width), b16),
+            shape((2, n_z, share, width), b16),
+            shape((n_shard, 2, n_z, w_share, width), b16),
+        ],
+        in_specs=vmem_specs(8),
+        out_specs=vmem_specs(3),
+        scratch_shapes=[
+            pltpu.VMEM((n_shard, width, width), b16),
+            pltpu.VMEM((n_shard, 2, neg_half, width), b16),
+            pltpu.VMEM((n_shard, 8, capacity), jnp.int32),
+            pltpu.VMEM((n_shard, 8, capacity), jnp.int32),
+            pltpu.VMEM((n_shard, capacity, width), b16),
+            pltpu.VMEM((n_shard, capacity, width), b16),
+            pltpu.VMEM((rows_count, width), b16),
+            pltpu.VMEM((4, tok_rows, width), f32),
+            pltpu.VMEM((4, tok_rows, width), b16),
+            pltpu.VMEM((HEADS, tok_rows, tok_rows), f32),
+            pltpu.VMEM((tok_rows, tok_rows), f32),
+            pltpu.VMEM((tok_rows, width), b16),
+            pltpu.VMEM((tok_rows, width), b16),
+            pltpu.VMEM((tok_rows, width), b16),
+            pltpu.VMEM((tok_rows, width), f32),
+            pltpu.VMEM((4, tok_rows, width), b16),
+            pltpu.VMEM((parts, n_shard, capacity, cols), b16),
+            pltpu.VMEM((parts, n_shard, capacity, cols), b16),
+            pltpu.VMEM((2, parts, n_shard, neg_half + w_half, cols), b16),
+            pltpu.VMEM((parts, n_shard, neg_half + w_half, cols), b16),
+            pltpu.VMEM((parts, n_shard, neg_half + w_half, cols), b16),
+            pltpu.VMEM((parts, n_shard, neg_half + w_half, cols), b16),
+            pltpu.VMEM((parts, 2, n_z, share, cols), b16),
+            pltpu.VMEM((parts, n_z, share, cols), b16),
+            pltpu.VMEM((parts, n_z, share + w_share, cols), b16),
+            pltpu.VMEM((parts, n_z, share + w_share, cols), b16),
+            pltpu.SemaphoreType.DMA((copies,)),
+            pltpu.SemaphoreType.DMA((copies,)),
+        ],
+        compiler_params=pltpu.CompilerParams(
+            collective_id=0, has_side_effects=True, vmem_limit_bytes=56 * 2**20
+        ),
+        name="layer",
+    )(
+        tokens,
+        w_proj,
+        w_out,
+        item_rows,
+        lengths,
+        target_owner,
+        target_row.reshape(1, -1),
+        negative_rows.reshape(1, -1),
+    )
+    item_grads = gathered.transpose(1, 0, 2, 3).reshape(rows_count, width).astype(f32)
+    return (grad_tokens, w_gathered.reshape(width, width).astype(f32), item_grads)
+
+
+def fits_kernels(mesh):
+    n_dp, n_shard = mesh.shape["dp"], mesh.shape["shard"]
+    return n_dp % 2 == 0 and n_dp > 2 and n_shard == 4 and D % (16 * n_dp * n_shard) == 0
+
+
 def solution(mesh):
     in_specs = (
         P(("dp", "shard"), None),
@@ -244,4 +760,6 @@
         P("shard"),
     )
     out_specs = (P(("dp", "shard"), None), P(), P("shard", None))
-    return jax.shard_map(shards, mesh=mesh, in_specs=in_specs, out_specs=out_specs, check_vma=False)
+    return jax.shard_map(
+        shards if fits_kernels(mesh) else plain_shards,
+        mesh=mesh, in_specs=in_specs, out_specs=out_specs, check_vma=False)

time: 328 us -> 80.6 us (0.25)
  waiting for transfers between devices: 182 us -> 0 us
  Pallas kernels: 0 us -> 71.5 us
  other arithmetic: 44.8 us -> 2.64 us
  matrix products: 37.9 us -> 0 us
  blocking collectives: 22.2 us -> 0 us
  between operations: 14.3 us -> 0.67 us
  starting transfers between devices: 11.8 us -> 0 us
  local copies, waits for them, and re-layouts: 13.1 us -> 5.06 us
    psum x1 -> x0, waiting for transfers between devices: 128 us -> none  [shards(): weight_grads = lax.psum(weight_part, ('dp', 'shard')) / loss_scale]
    pallas_call x0 -> x1, Pallas kernels: none -> 71.5 us  [shards(): pl.pallas_call(functools.partial(layer_kernel, n_dp, n_shard, capacity),...]
    dot_general x32 -> x0, matrix products: 37.9 us -> none  [the longest x11 14.5 us: reduce_last_dimension(): lax.dot_general(operand, other_side, (((1,), (1,)), ((), ())), preferred_...]
    reduce_scatter x2 -> x0, waiting for transfers between devices: 25.9 us -> none  [the longest x1 15.2 us: shards(): lax.psum_scatter(grad_items.astype(jnp.bfloat16), 'dp', scatter_dimension...]
    all_gather x2 -> x0, waiting for transfers between devices: 23.4 us -> none  [the longest x1 23.4 us: shards(): lax.all_gather(finish_rows(summed_share, share_wide).astype(jnp.bfloat16)...]
    all_gather x1 -> x0, blocking collectives: 22.2 us -> none  [shards(): lax.all_gather(jnp.take(unit_items, negative_rows, axis=0), 'shard', axis...]
    scatter-add x2 -> x0, other arithmetic: 13.1 us -> none  [the longest x1 8.93 us: shards(): grad_items = jnp.zeros((item_rows.shape[0], model_width), jnp.float32).at...]
    all_to_all x3 -> x0, starting transfers between devices: 11.4 us -> none  [the longest x1 4.33 us: shards(): lax.all_to_all(outgoing.reshape(shard_count, capacity, model_width).astyp...]
  transfers between devices with their start and end apart: 8 -> 0, of which waited for: 5 -> 0; matrix products, arithmetic and copies ran while one was open for 19% -> 0% of each run, Pallas kernels for 0% -> 0%
where the time goes in v2:
time: 80.6 us; the launch traced here: 79.9 us
  Pallas kernels  71.5 us (89%)
  local copies, waits for them, and re-layouts  5.06 us (6%)
  other arithmetic  2.64 us (3%)
    pallas_call x1, Pallas kernels, shards(): pl.pallas_call(functools.partial(layer_kernel, n_dp, n_shard, capacity),...  71.5 us
    unnamed x6, local copies, waits for them, and re-layouts  2.25 us

profile of v2, /device:TPU:9, one launch (start us, length us, event | category | flops | bytes accessed | tf_op | source)
XLA Modules:
  0.0 79.9 jit_solution(17727350723908558689)
XLA Ops:
  0.6 1.5 %copy.12.owner_ref = s32[384,1]{1,0:T(8,128)} copy(s32[384,1]{0,1:T(1,128)} %param.13) | data formatting | bytes 3072 | tf_op args[5]
  2.1 1.2 %reshape.18.target_ref = s32[1,384]{1,0:T(1,128)} reshape(s32[384]{0:T(512)} %param.14) | data formatting | bytes 3072 | tf_op jit(solution)/shard_map/reshape | solution.py:739
  3.4 71.5 %layer.1 = (bf16[384,512]{1,0:T(8,128)(2,1)}, bf16[2,4,128,512]{3,2,1,0:T(8,128)(2,1)}, bf16[4,2,4,16,512]{4,3,2,1,0:T(8,128)(2,1)}) custom-call(bf16[384,512]{1,0:T(8,128)(2,1)} %tokens_ref.1, bf16[512,512]{1,0:T(8,128)(2,1)} %w_ref.1, bf16[512,512]{1,0:T(8,128)(2,1)} %w_out_ref.1, bf16[1024,512]{1,0:T(8,128)(2,1)} %items_ref.1, s32[1,4]{1,0:T(1,128)} %lengths_ref.1, ...), custom_call_target="tpu_custom_call" | custom-call | tf_op jit(solution)/shard_map/layer/pallas_call | solution.py:689
  74.9 1.5 %convert_bitcast_fusion = f32[4,2,128,512]{3,2,0,1:T(8,128)S(1)} fusion(bf16[2,4,128,512]{3,2,1,0:T(8,128)(2,1)} %get-tuple-element.8), kind=kLoop, calls=%fused_computation | loop fusion | flops 524288 | bytes 3145728 | tf_op jit(solution)/shard_map/convert_element_type | solution.py:742
  76.4 0.0 copy-start
  76.4 0.0 copy-start.1
  76.4 1.6 %copy.13 = f32[4,2,128,512]{3,2,1,0:T(8,128)} copy(f32[4,2,128,512]{3,2,0,1:T(8,128)S(1)} %convert_bitcast_fusion) | data formatting | bytes 4194304 | tf_op jit(solution)/shard_map/convert_element_type | solution.py:742
  78.0 0.0 copy-done
  78.0 1.1 %bitcast_convert_fusion = f32[512,512]{1,0:T(8,128)} fusion(bf16[4,2,4,16,512]{4,3,2,1,0:T(8,128)(2,1)S(1)} %copy-done), kind=kLoop, calls=%fused_computation.1 | loop fusion | flops 262144 | bytes 1572864 | tf_op jit(solution)/shard_map/convert_element_type | solution.py:743
  79.1 0.0 copy-done.1
  79.1 0.7 copy.15
Async XLA Ops:
  76.4 1.6 %copy-start = (bf16[4,2,4,16,512]{4,3,2,1,0:T(8,128)(2,1)S(1)}, bf16[4,2,4,16,512]{4,3,2,1,0:T(8,128)(2,1)}, u32[]{:S(2)}) copy-start(bf16[4,2,4,16,512]{4,3,2,1,0:T(8,128)(2,1)} %get-tuple-element.7) | copy-start | bytes 1572868
  76.4 2.7 %copy-start.1 = (bf16[384,512]{1,0:T(8,128)(2,1)S(1)}, bf16[384,512]{1,0:T(8,128)(2,1)}, u32[]{:S(2)}) copy-start(bf16[384,512]{1,0:T(8,128)(2,1)} %get-tuple-element.12) | copy-start | bytes 1179652

commit v3 on v2

--- a/solution.py
+++ b/solution.py
@@ -350,6 +350,14 @@
     in_pair,
     out_z,
     in_z,
+    slots_back,
+    picks_ref,
+    w_pair,
+    w_pair_in,
+    w_out_z,
+    w_in_z,
+    w_out_shard,
+    w_in_shard,
     send_sem,
     recv_sem,
 ):
@@ -377,23 +385,24 @@
     half = w_ref.shape[0] // 2
     share = rows_count // n_dp
     w_rows = width // n_shard
-    w_half = w_rows // 2
-    w_share = w_half // n_z
+    w_share = w_rows // n_dp
     n_parts, part_cols = out_rows.shape[0], out_rows.shape[-1]
 
-    owner_col = owner_ref[...]
+    owner_row = owner_ref[...]
+    owner_col = as_column(owner_row)
     token_a = lax.broadcasted_iota(jnp.int32, (tok_rows, tok_rows), 0)
     token_b = lax.broadcasted_iota(jnp.int32, (tok_rows, tok_rows), 1)
-    same = (as_row(owner_col) == owner_col) & (token_b < token_a)
+    same = (owner_row == owner_col) & (token_b < token_a)
     slot = jnp.sum(jnp.where(same, 1.0, 0.0), axis=1, keepdims=True).astype(jnp.int32)
     position = owner_col * capacity + slot
     slots = one_hot_columns(position, n_shard * capacity)
-    target = as_column(target_ref[...])
+    target = as_column(target_ref[...].reshape(1, -1))
     request = jnp.sum(jnp.where(slots, target, 0), axis=0, keepdims=True)
     for j in range(n_shard):
         part = request[:, j * capacity : (j + 1) * capacity]
         requests[j] = jnp.broadcast_to(part, (8, capacity))
     slots_one = ones_of(slots)
+    slots_back[...] = row_picks(as_row(position), n_shard * capacity)
 
     pl.semaphore_wait(barrier, len(greeted))
     ask_copies = [send(requests.at[peer[1]], asked.at[shard], peer) for peer in peers]
@@ -404,7 +413,8 @@
     rows_wide = items_ref[...].astype(jnp.float32)
     item_scale = lax.rsqrt(jnp.sum(rows_wide * rows_wide, axis=1, keepdims=True) + epsilon)
     unit[...] = (rows_wide * item_scale).astype(jnp.bfloat16)
-    negative_col = as_column(negative_ref[...])
+    negative_row = negative_ref[...]
+    negative_col = as_column(negative_row)
     own_negatives = jnp.dot(
         ones_of(one_hot_columns(negative_col, rows_count)),
         unit[...],
@@ -425,13 +435,17 @@
         pre[j] = values
         act[j] = (values * lax.logistic(values)).astype(jnp.bfloat16)
 
+    def rows_for(source):
+        asked_row = asked[source][0:1]
+        picks_ref[source] = row_picks(asked_row, rows_count)
+        picks = ones_of(one_hot_columns(as_column(asked_row), rows_count))
+        return jnp.dot(picks, unit[...], preferred_element_type=jnp.float32).astype(jnp.bfloat16)
+
     section(shard)
     for k, source in enumerate(others):
         ask_copies[k].wait_recv()
-        picks = row_picks(asked[source][0:1], rows_count)
-        served[source] = contract_first(picks, unit[...]).astype(jnp.bfloat16)
-    picks = row_picks(requests[shard][0:1], rows_count)
-    fetched[shard] = contract_first(picks, unit[...]).astype(jnp.bfloat16)
+        served[source] = rows_for(source)
+    fetched[shard] = rows_for(shard)
     w_pairs = []
     for k, source in enumerate(others):
         w_copies[k].wait_recv()
@@ -496,9 +510,10 @@
     row_sends = []
     for h in range(n_parts):
         for j in range(n_shard):
-            out_rows[h, j] = contract_first(
-                slots_one[:, j * capacity : (j + 1) * capacity],
+            out_rows[h, j] = jnp.dot(
+                slots_back[j * capacity : (j + 1) * capacity],
                 grad_target[:, h * part_cols : (h + 1) * part_cols],
+                preferred_element_type=jnp.float32,
             ).astype(jnp.bfloat16)
         if h == 0:
             row_sends.append(
@@ -519,16 +534,20 @@
     grad_out_ref[...] = grad_out
     grad_out_b = grad_out.astype(jnp.bfloat16)
     neg_part = contract_first(negative_probs, unit_b).astype(jnp.bfloat16)
-    w_part = contract_first(gated, grad_out_b).astype(jnp.bfloat16)
     for h in range(n_parts):
         cols = slice(h * part_cols, (h + 1) * part_cols)
         for j in range(n_shard):
             for c in range(2):
                 first = (2 * j + c) * neg_half
-                pair_sums[c, h, j, 0:neg_half] = neg_part[first : first + neg_half, cols]
-                first = (2 * j + c) * w_half
-                pair_sums[c, h, j, neg_half:] = w_part[first : first + w_half, cols]
+                pair_sums[c, h, j] = neg_part[first : first + neg_half, cols]
     sum_pair = send(pair_sums.at[1 - core], pair_in, sibling)
+    w_part = contract_first(gated, grad_out_b).astype(jnp.bfloat16)
+    for c in range(2):
+        for j in range(n_shard):
+            for z in range(n_z):
+                first = ((c * n_shard + j) * n_z + z) * w_share
+                w_pair[c, z, j] = w_part[first : first + w_share]
+    w_pair_copy = send(w_pair.at[1 - core], w_pair_in, sibling)
     sum_pair.wait_recv()
     out_sums[...] = (
         pair_sums[core].astype(jnp.float32) + pair_in[...].astype(jnp.float32)
@@ -542,6 +561,13 @@
         sum_sends.append(
             [send(out_sums.at[h, peer[1]], in_sums.at[h, shard], peer) for peer in peers]
         )
+    w_pair_copy.wait_recv()
+    w_out_z[...] = (
+        w_pair[core].astype(jnp.float32) + w_pair_in[...].astype(jnp.float32)
+    ).astype(jnp.bfloat16)
+    w_z_sends = [
+        send(w_out_z.at[z_to[k]], w_in_z.at[height], peer) for k, peer in enumerate(z_peers)
+    ]
 
     grad_gated = reduce_last_dimension(grad_out_b, w_out_ref[...])
     grad_pre[0] = (grad_gated * joined_wide * middle_scale * silu_slope(pre[0])).astype(
@@ -577,33 +603,31 @@
 
     def collect(h):
         grad_items = jnp.zeros((rows_count, part_cols), jnp.float32)
-        sums = jnp.zeros((neg_half + w_half, part_cols), jnp.float32)
+        sums = jnp.zeros((neg_half, part_cols), jnp.float32)
         for k, source in enumerate([shard] + others):
             if k > 0:
                 row_sends[h][k - 1].wait_recv()
                 sum_sends[h][k - 1].wait_recv()
             rows = out_rows[h, shard] if k == 0 else in_rows[h, source]
             part = out_sums[h, shard] if k == 0 else in_sums[h, source]
-            picks = row_picks(asked[source][0:1], rows_count)
-            grad_items += jnp.dot(picks, rows, preferred_element_type=jnp.float32)
+            grad_items += jnp.dot(picks_ref[source], rows, preferred_element_type=jnp.float32)
             sums += part.astype(jnp.float32)
-        rows = lax.broadcasted_iota(jnp.int32, (neg_half, rows_count), 1)
-        own_rows = jnp.where(core == 0, negative_col[:neg_half], negative_col[neg_half:])
-        grad_items += contract_first(
-            ones_of(rows == own_rows), sums[0:neg_half].astype(jnp.bfloat16)
+        own_rows = jnp.where(core == 0, negative_row[:, :neg_half], negative_row[:, neg_half:])
+        grad_items += jnp.dot(
+            row_picks(own_rows, rows_count),
+            sums.astype(jnp.bfloat16),
+            preferred_element_type=jnp.float32,
         )
         for z in range(n_z):
             for c in range(2):
                 d = z * 2 + c
                 out_pair[h, c, z] = grad_items[d * share : (d + 1) * share].astype(jnp.bfloat16)
-            first = neg_half + z * w_share
-            out_z[h, z, share:] = sums[first : first + w_share].astype(jnp.bfloat16)
         return send(out_pair.at[h, 1 - core], in_pair.at[h], sibling)
 
     def pass_on(h, pair):
         pair.wait_recv()
         for z in range(n_z):
-            out_z[h, z, 0:share] = (
+            out_z[h, z] = (
                 out_pair[h, core, z].astype(jnp.float32) + in_pair[h, z].astype(jnp.float32)
             ).astype(jnp.bfloat16)
         return [
@@ -614,12 +638,29 @@
     pair = collect(0)
     head_back(1)
     z_sends = [pass_on(0, pair)]
-    for h in range(1, n_parts):
-        pair = collect(h)
-        head_back(2)
-        z_sends.append(pass_on(h, pair))
-    for head in range(3 if n_parts > 1 else 2, HEADS):
+    w_total = w_out_z[height].astype(jnp.float32)
+    for k, z in enumerate(z_from):
+        w_z_sends[k].wait_recv()
+        w_total += w_in_z[z].astype(jnp.float32)
+    w_out_shard[...] = w_total.astype(jnp.bfloat16)
+    w_sends = [send(w_out_shard.at[peer[1]], w_in_shard.at[shard], peer) for peer in peers]
+    pair = collect(1)
+    head_back(2)
+    z_sends.append(pass_on(1, pair))
+    w_total = w_out_shard[shard].astype(jnp.float32)
+    for k, source in enumerate(others):
+        w_sends[k].wait_recv()
+        w_total += w_in_shard[source].astype(jnp.float32)
+    w_gathered[core, shard, height] = (w_total / loss_scale).astype(jnp.bfloat16)
+    w_mine = w_gathered.at[core, shard, height]
+    w_z = [send(w_mine, w_mine, peer) for peer in z_peers]
+    for head in range(3, HEADS):
         head_back(head)
+    for copy in w_z:
+        copy.wait_recv()
+    w_block = w_gathered.at[core, shard]
+    w_around = [send(w_block, w_block, peer) for peer in peers]
+    last = [send(w_block, w_block, sibling)]
     grad_normed = jnp.zeros((tok_rows, width), jnp.float32)
     for j in range(n_shard):
         grad_normed += reduce_last_dimension(grad_pre[j], w_full[j])
@@ -637,27 +678,19 @@
             total += in_z[h, z].astype(jnp.float32)
         totals_parts.append(total)
     total = jnp.concatenate(totals_parts, axis=1)
-    w_gathered[shard, core, height] = (total[share:] / loss_scale).astype(jnp.bfloat16)
-    w_mine = w_gathered.at[shard, core, height]
-    w_z = [send(w_mine, w_mine, peer) for peer in z_peers]
     own = pl.ds(pl.multiple_of(dp * share, share), share)
-    finished = finish_rows(total[0:share], items_ref[own].astype(jnp.float32))
-    gathered[core, height] = finished.astype(jnp.bfloat16)
-    items_mine = gathered.at[core, height]
+    finished = finish_rows(total, items_ref[own].astype(jnp.float32))
+    gathered[height, core] = finished.astype(jnp.bfloat16)
+    items_mine = gathered.at[height, core]
     items_z = [send(items_mine, items_mine, peer) for peer in z_peers]
-    last = [send(items_mine, items_mine, sibling)]
-    for copy in w_z:
-        copy.wait_recv()
-    w_block = w_gathered.at[shard, core]
-    w_around = [send(w_block, w_block, peer) for peer in peers]
-    last.append(send(w_block, w_block, sibling))
+    last.append(send(items_mine, items_mine, sibling))
     for k, source in enumerate(others):
         w_around[k].wait_recv()
-        piece = w_gathered.at[source, core]
+        piece = w_gathered.at[core, source]
         last.append(send(piece, piece, sibling))
     for k, z in enumerate(z_from):
         items_z[k].wait_recv()
-        piece = gathered.at[core, z]
+        piece = gathered.at[z, core]
         last.append(send(piece, piece, sibling))
     for copy in last:
         copy.wait_recv()
@@ -690,8 +723,8 @@
         functools.partial(layer_kernel, n_dp, n_shard, capacity),
         out_shape=[
             shape((tok_rows, width), b16),
-            shape((2, n_z, share, width), b16),
-            shape((n_shard, 2, n_z, w_share, width), b16),
+            shape((n_z, 2, share, width), b16),
+            shape((2, n_shard, n_z, w_share, width), b16),
         ],
         in_specs=vmem_specs(8),
         out_specs=vmem_specs(3),
@@ -714,14 +747,22 @@
             pltpu.VMEM((4, tok_rows, width), b16),
             pltpu.VMEM((parts, n_shard, capacity, cols), b16),
             pltpu.VMEM((parts, n_shard, capacity, cols), b16),
-            pltpu.VMEM((2, parts, n_shard, neg_half + w_half, cols), b16),
-            pltpu.VMEM((parts, n_shard, neg_half + w_half, cols), b16),
-            pltpu.VMEM((parts, n_shard, neg_half + w_half, cols), b16),
-            pltpu.VMEM((parts, n_shard, neg_half + w_half, cols), b16),
+            pltpu.VMEM((2, parts, n_shard, neg_half, cols), b16),
+            pltpu.VMEM((parts, n_shard, neg_half, cols), b16),
+            pltpu.VMEM((parts, n_shard, neg_half, cols), b16),
+            pltpu.VMEM((parts, n_shard, neg_half, cols), b16),
             pltpu.VMEM((parts, 2, n_z, share, cols), b16),
             pltpu.VMEM((parts, n_z, share, cols), b16),
-            pltpu.VMEM((parts, n_z, share + w_share, cols), b16),
-            pltpu.VMEM((parts, n_z, share + w_share, cols), b16),
+            pltpu.VMEM((parts, n_z, share, cols), b16),
+            pltpu.VMEM((parts, n_z, share, cols), b16),
+            pltpu.VMEM((n_shard * capacity, tok_rows), b16),
+            pltpu.VMEM((n_shard, rows_count, capacity), b16),
+            pltpu.VMEM((2, n_z, n_shard, w_share, width), b16),
+            pltpu.VMEM((n_z, n_shard, w_share, width), b16),
+            pltpu.VMEM((n_z, n_shard, w_share, width), b16),
+            pltpu.VMEM((n_z, n_shard, w_share, width), b16),
+            pltpu.VMEM((n_shard, w_share, width), b16),
+            pltpu.VMEM((n_shard, w_share, width), b16),
             pltpu.SemaphoreType.DMA((copies,)),
             pltpu.SemaphoreType.DMA((copies,)),
         ],
@@ -735,11 +776,11 @@
         w_out,
         item_rows,
         lengths,
-        target_owner,
-        target_row.reshape(1, -1),
+        target_owner.reshape(1, -1),
+        target_row,
         negative_rows.reshape(1, -1),
     )
-    item_grads = gathered.transpose(1, 0, 2, 3).reshape(rows_count, width).astype(f32)
+    item_grads = gathered.reshape(rows_count, width).astype(f32)
     return (grad_tokens, w_gathered.reshape(width, width).astype(f32), item_grads)
 
 

time: 80.6 us -> 78.7 us (0.976)
  local copies, waits for them, and re-layouts: 5.06 us -> 0.75 us
  Pallas kernels: 71.5 us -> 73 us
  other arithmetic: 2.64 us -> 4.05 us
    convert_element_type x1 -> x0, local copies, waits for them, and re-layouts: 1.56 us -> none  [shards(): gathered.transpose(1, 0, 2, 3).reshape(rows_count, width).astype(f32)]
    pallas_call x1, Pallas kernels: 71.5 us -> 73 us  [shards(): pl.pallas_call(functools.partial(layer_kernel, n_dp, n_shard, capacity),...]
    unnamed x6 -> x5, local copies, waits for them, and re-layouts: 2.25 us -> 0.75 us
    convert_element_type x1, other arithmetic: 1.5 us -> 2.91 us  [shards(): item_grads = gathered.reshape(rows_count, width).astype(f32)]
    reshape x1 -> x0, local copies, waits for them, and re-layouts: 1.24 us -> none  [shards(): target_row.reshape(1, -1)]
where the time goes in v3:
time: 78.7 us; the launch traced here: 78.5 us
  Pallas kernels  73 us (93%)
  other arithmetic  4.05 us (5%)
    pallas_call x1, Pallas kernels, shards(): pl.pallas_call(functools.partial(layer_kernel, n_dp, n_shard, capacity),...  73 us
    convert_element_type x1, other arithmetic, shards(): item_grads = gathered.reshape(rows_count, width).astype(f32)  2.91 us

profile of v3, /device:TPU:9, one launch (start us, length us, event | category | flops | bytes accessed | tf_op | source)
XLA Modules:
  0.0 78.5 jit_solution(3234004679965820407)
XLA Ops:
  0.6 73.0 %layer.1 = (bf16[384,512]{1,0:T(8,128)(2,1)}, bf16[4,2,128,512]{3,2,1,0:T(8,128)(2,1)}, bf16[2,4,4,16,512]{4,3,2,1,0:T(8,128)(2,1)}) custom-call(bf16[384,512]{1,0:T(8,128)(2,1)} %tokens_ref.1, bf16[512,512]{1,0:T(8,128)(2,1)} %w_ref.1, bf16[512,512]{1,0:T(8,128)(2,1)} %w_out_ref.1, bf16[1024,512]{1,0:T(8,128)(2,1)} %items_ref.1, s32[1,4]{1,0:T(1,128)} %lengths_ref.1, ...), custom_call_target="tpu_custom_call" | custom-call | tf_op jit(solution)/shard_map/layer/pallas_call | solution.py:722
  73.7 0.0 copy-start
  73.7 0.0 copy-start.1
  73.7 2.9 %bitcast_convert_fusion = f32[1024,512]{1,0:T(8,128)} fusion(bf16[4,2,128,512]{3,2,1,0:T(8,128)(2,1)} %get-tuple-element.8), kind=kLoop, calls=%fused_computation | loop fusion | flops 524288 | bytes 3145728 | tf_op jit(solution)/shard_map/convert_element_type | solution.py:783
  76.6 0.0 copy-done
  76.6 1.1 %bitcast_convert_fusion.1 = f32[512,512]{1,0:T(8,128)} fusion(bf16[2,4,4,16,512]{4,3,2,1,0:T(8,128)(2,1)S(1)} %copy-done), kind=kLoop, calls=%fused_computation.1 | loop fusion | flops 262144 | bytes 1572864 | tf_op jit(solution)/shard_map/convert_element_type | solution.py:784
  77.8 0.0 copy-done.1
  77.8 0.7 copy.12
Async XLA Ops:
  73.7 2.9 %copy-start = (bf16[2,4,4,16,512]{4,3,2,1,0:T(8,128)(2,1)S(1)}, bf16[2,4,4,16,512]{4,3,2,1,0:T(8,128)(2,1)}, u32[]{:S(2)}) copy-start(bf16[2,4,4,16,512]{4,3,2,1,0:T(8,128)(2,1)} %get-tuple-element.7) | copy-start | bytes 1572868
  73.7 4.1 %copy-start.1 = (bf16[384,512]{1,0:T(8,128)(2,1)S(1)}, bf16[384,512]{1,0:T(8,128)(2,1)}, u32[]{:S(2)}) copy-start(bf16[384,512]{1,0:T(8,128)(2,1)} %get-tuple-element.12) | copy-start | bytes 1179652

commit v4 on v3

--- a/solution.py
+++ b/solution.py
@@ -378,6 +378,11 @@
         started.append(copy)
         return copy
 
+    def left(copies):
+        for copy in copies:
+            copy.wait_send()
+            started[:] = [other for other in started if other is not copy]
+
     rows_count, width = items_ref.shape
     tok_rows = tokens_ref.shape[0]
     neg_rows = negative_ref.shape[1]
@@ -388,6 +393,15 @@
     w_share = w_rows // n_dp
     n_parts, part_cols = out_rows.shape[0], out_rows.shape[-1]
 
+    pl.semaphore_wait(barrier, len(greeted))
+    edge = half // 4
+    first_row = core * half
+    odd = lax.rem(height, 2)
+    partner = ((height + 1 - 2 * odd) * 2 + core, shard)
+    rows_a = pl.ds(pl.multiple_of(first_row + odd * edge, edge), edge)
+    rows_b = pl.ds(pl.multiple_of(first_row + (1 - odd) * edge, edge), edge)
+    rows_c = pl.ds(pl.multiple_of(first_row + 2 * edge, edge), half - 2 * edge)
+    a_copies = [send(w_ref.at[rows_a], w_full.at[shard, rows_a], peer) for peer in peers]
     owner_row = owner_ref[...]
     owner_col = as_column(owner_row)
     token_a = lax.broadcasted_iota(jnp.int32, (tok_rows, tok_rows), 0)
@@ -404,10 +418,16 @@
     slots_one = ones_of(slots)
     slots_back[...] = row_picks(as_row(position), n_shard * capacity)
 
-    pl.semaphore_wait(barrier, len(greeted))
     ask_copies = [send(requests.at[peer[1]], asked.at[shard], peer) for peer in peers]
-    mine = pl.ds(pl.multiple_of(core * half, half), half)
-    w_copies = [send(w_ref.at[mine], w_full.at[shard, mine], peer) for peer in peers]
+    left(a_copies)
+    c_copies = [send(w_ref.at[rows_c], w_full.at[shard, rows_c], peer) for peer in peers]
+    w_pairs = []
+    b_copies = []
+    for k, source in enumerate(others):
+        a_copies[k].wait_recv()
+        piece = w_full.at[source, rows_a]
+        b_copies.append(send(piece, piece, partner))
+        w_pairs.append(send(piece, piece, sibling))
     asked[shard] = requests[shard]
 
     rows_wide = items_ref[...].astype(jnp.float32)
@@ -446,21 +466,23 @@
         ask_copies[k].wait_recv()
         served[source] = rows_for(source)
     fetched[shard] = rows_for(shard)
-    w_pairs = []
-    for k, source in enumerate(others):
-        w_copies[k].wait_recv()
-        piece = w_full.at[source, mine]
-        w_pairs.append(send(piece, piece, sibling))
+    left(c_copies)
     row_copies = [
         send(served.at[source], fetched.at[shard], (dp, source)) for source in others
     ]
+    for rows, arriving in ((rows_c, c_copies), (rows_b, b_copies)):
+        for k, source in enumerate(others):
+            arriving[k].wait_recv()
+            piece = w_full.at[source, rows]
+            w_pairs.append(send(piece, piece, sibling))
     neg_pairs = []
     for k, source in enumerate(others):
         neg_copies[k].wait_recv()
         piece = negatives.at[source, core]
         neg_pairs.append(send(piece, piece, sibling))
     for k, source in enumerate(others):
-        w_pairs[k].wait_recv()
+        for copy in w_pairs[k :: n_shard - 1]:
+            copy.wait_recv()
         section(source)
 
     def head_part(j, head):
@@ -636,8 +658,8 @@
 
     head_back(0)
     pair = collect(0)
+    z_sends = [pass_on(0, pair)]
     head_back(1)
-    z_sends = [pass_on(0, pair)]
     w_total = w_out_z[height].astype(jnp.float32)
     for k, z in enumerate(z_from):
         w_z_sends[k].wait_recv()
@@ -786,7 +808,7 @@
 
 def fits_kernels(mesh):
     n_dp, n_shard = mesh.shape["dp"], mesh.shape["shard"]
-    return n_dp % 2 == 0 and n_dp > 2 and n_shard == 4 and D % (16 * n_dp * n_shard) == 0
+    return n_dp % 2 == 0 and n_dp > 2 and n_shard == 4 and n_dp % 4 == 0 and D % (16 * n_dp * n_shard) == 0
 
 
 def solution(mesh):

time: 78.7 us -> 74.7 us (0.949)
  Pallas kernels: 73 us -> 69.1 us
    pallas_call x1, Pallas kernels: 73 us -> 69.1 us  [shards(): pl.pallas_call(functools.partial(layer_kernel, n_dp, n_shard, capacity),...]
where the time goes in v4:
time: 74.7 us; the launch traced here: 74.6 us
  Pallas kernels  69.1 us (93%)
  other arithmetic  4.05 us (5%)
  local copies, waits for them, and re-layouts  0.75 us (1%)
    pallas_call x1, Pallas kernels, shards(): pl.pallas_call(functools.partial(layer_kernel, n_dp, n_shard, capacity),...  69.1 us
    convert_element_type x1, other arithmetic, shards(): item_grads = gathered.reshape(rows_count, width).astype(f32)  2.91 us

profile of v4, /device:TPU:9, one launch (start us, length us, event | category | flops | bytes accessed | tf_op | source)
XLA Modules:
  0.0 74.6 jit_solution(8488393905197009633)
XLA Ops:
  0.6 69.1 %layer.1 = (bf16[384,512]{1,0:T(8,128)(2,1)}, bf16[4,2,128,512]{3,2,1,0:T(8,128)(2,1)}, bf16[2,4,4,16,512]{4,3,2,1,0:T(8,128)(2,1)}) custom-call(bf16[384,512]{1,0:T(8,128)(2,1)} %tokens_ref.1, bf16[512,512]{1,0:T(8,128)(2,1)} %w_ref.1, bf16[512,512]{1,0:T(8,128)(2,1)} %w_out_ref.1, bf16[1024,512]{1,0:T(8,128)(2,1)} %items_ref.1, s32[1,4]{1,0:T(1,128)} %lengths_ref.1, ...), custom_call_target="tpu_custom_call" | custom-call | tf_op jit(solution)/shard_map/layer/pallas_call | solution.py:744
  69.7 0.0 copy-start
  69.8 0.0 copy-start.1
  69.8 2.9 %bitcast_convert_fusion = f32[1024,512]{1,0:T(8,128)} fusion(bf16[4,2,128,512]{3,2,1,0:T(8,128)(2,1)} %get-tuple-element.8), kind=kLoop, calls=%fused_computation | loop fusion | flops 524288 | bytes 3145728 | tf_op jit(solution)/shard_map/convert_element_type | solution.py:805
  72.7 0.0 copy-done
  72.7 1.1 %bitcast_convert_fusion.1 = f32[512,512]{1,0:T(8,128)} fusion(bf16[2,4,4,16,512]{4,3,2,1,0:T(8,128)(2,1)S(1)} %copy-done), kind=kLoop, calls=%fused_computation.1 | loop fusion | flops 262144 | bytes 1572864 | tf_op jit(solution)/shard_map/convert_element_type | solution.py:806
  73.8 0.0 copy-done.1
  73.8 0.7 %copy.12 = bf16[384,512]{1,0:T(8,128)(2,1)} copy(bf16[384,512]{1,0:T(8,128)(2,1)S(1)} %copy-done.1) | data formatting | bytes 786432
Async XLA Ops:
  69.7 2.9 %copy-start = (bf16[2,4,4,16,512]{4,3,2,1,0:T(8,128)(2,1)S(1)}, bf16[2,4,4,16,512]{4,3,2,1,0:T(8,128)(2,1)}, u32[]{:S(2)}) copy-start(bf16[2,4,4,16,512]{4,3,2,1,0:T(8,128)(2,1)} %get-tuple-element.7) | copy-start | bytes 1572868
  69.8 4.1 %copy-start.1 = (bf16[384,512]{1,0:T(8,128)(2,1)S(1)}, bf16[384,512]{1,0:T(8,128)(2,1)}, u32[]{:S(2)}) copy-start(bf16[384,512]{1,0:T(8,128)(2,1)} %get-tuple-element.12) | copy-start | bytes 1179652

commit v5 on v4

--- a/solution.py
+++ b/solution.py
@@ -322,6 +322,8 @@
     target_ref,
     negative_ref,
     grad_tokens_ref,
+    item_grads_ref,
+    weight_grads_ref,
     gathered,
     w_gathered,
     w_full,
@@ -656,6 +658,23 @@
             send(out_z.at[h, z_to[k]], in_z.at[h, height], peer) for k, peer in enumerate(z_peers)
         ]
 
+    def share_out(h):
+        total = out_z[h, height].astype(jnp.float32)
+        for k, z in enumerate(z_from):
+            z_sends[h][k].wait_recv()
+            total += in_z[h, z].astype(jnp.float32)
+        gathered[h, height, core] = total.astype(jnp.bfloat16)
+        piece = gathered.at[h, height, core]
+        along = [send(piece, piece, peer) for peer in z_peers]
+        return along, [send(piece, piece, sibling)]
+
+    def finish(z, c):
+        rows = pl.ds(pl.multiple_of((z * 2 + c) * share, share), share)
+        total = jnp.concatenate([gathered[h, z, c] for h in range(n_parts)], axis=1)
+        item_grads_ref[rows] = finish_rows(
+            total.astype(jnp.float32), items_ref[rows].astype(jnp.float32)
+        )
+
     head_back(0)
     pair = collect(0)
     z_sends = [pass_on(0, pair)]
@@ -678,6 +697,7 @@
     w_z = [send(w_mine, w_mine, peer) for peer in z_peers]
     for head in range(3, HEADS):
         head_back(head)
+    shared = [share_out(0)]
     for copy in w_z:
         copy.wait_recv()
     w_block = w_gathered.at[core, shard]
@@ -692,30 +712,27 @@
     )
     grad_tokens_ref[...] = (grad_out_ref[...] + grad_input).astype(jnp.bfloat16)
 
-    totals_parts = []
-    for h in range(n_parts):
-        total = out_z[h, height].astype(jnp.float32)
-        for k, z in enumerate(z_from):
-            z_sends[h][k].wait_recv()
-            total += in_z[h, z].astype(jnp.float32)
-        totals_parts.append(total)
-    total = jnp.concatenate(totals_parts, axis=1)
-    own = pl.ds(pl.multiple_of(dp * share, share), share)
-    finished = finish_rows(total, items_ref[own].astype(jnp.float32))
-    gathered[height, core] = finished.astype(jnp.bfloat16)
-    items_mine = gathered.at[height, core]
-    items_z = [send(items_mine, items_mine, peer) for peer in z_peers]
-    last.append(send(items_mine, items_mine, sibling))
+    shared.append(share_out(1))
     for k, source in enumerate(others):
         w_around[k].wait_recv()
         piece = w_gathered.at[core, source]
         last.append(send(piece, piece, sibling))
-    for k, z in enumerate(z_from):
-        items_z[k].wait_recv()
-        piece = gathered.at[z, core]
-        last.append(send(piece, piece, sibling))
+    finish(height, core)
     for copy in last:
         copy.wait_recv()
+    weight_grads_ref[...] = w_gathered[...].astype(jnp.float32)
+    for h in range(n_parts):
+        along, pairs = shared[h]
+        for k, z in enumerate(z_from):
+            along[k].wait_recv()
+            piece = gathered.at[h, z, core]
+            pairs.append(send(piece, piece, sibling))
+    for z in z_from:
+        finish(z, core)
+    for k, z in enumerate([height] + z_from):
+        for along, pairs in shared:
+            pairs[k].wait_recv()
+        finish(z, 1 - core)
     for copy in started:
         copy.wait_send()
 
@@ -741,16 +758,18 @@
     f32 = jnp.float32
     shape = jax.ShapeDtypeStruct
     copies = 7 * (n_shard - 1) + 4 * parts * (n_shard + n_z) + 2 * (n_shard + n_z) + 8
-    grad_tokens, gathered, w_gathered = pl.pallas_call(
+    grad_tokens, item_grads, weight_grads = pl.pallas_call(
         functools.partial(layer_kernel, n_dp, n_shard, capacity),
         out_shape=[
             shape((tok_rows, width), b16),
-            shape((n_z, 2, share, width), b16),
-            shape((2, n_shard, n_z, w_share, width), b16),
+            shape((rows_count, width), f32),
+            shape((2, n_shard, n_z, w_share, width), f32),
         ],
         in_specs=vmem_specs(8),
         out_specs=vmem_specs(3),
         scratch_shapes=[
+            pltpu.VMEM((parts, n_z, 2, share, cols), b16),
+            pltpu.VMEM((2, n_shard, n_z, w_share, width), b16),
             pltpu.VMEM((n_shard, width, width), b16),
             pltpu.VMEM((n_shard, 2, neg_half, width), b16),
             pltpu.VMEM((n_shard, 8, capacity), jnp.int32),
@@ -802,8 +821,7 @@
         target_row,
         negative_rows.reshape(1, -1),
     )
-    item_grads = gathered.reshape(rows_count, width).astype(f32)
-    return (grad_tokens, w_gathered.reshape(width, width).astype(f32), item_grads)
+    return (grad_tokens, weight_grads.reshape(width, width), item_grads)
 
 
 def fits_kernels(mesh):

time: 74.7 us -> 73.1 us (0.979); the launches traced: 74.6 us -> 72.1 us
  local copies, waits for them, and re-layouts: 0.75 us -> 5.5 us
  other arithmetic: 4.05 us -> 0 us
  Pallas kernels: 69.1 us -> 65.9 us
    unnamed x5, local copies, waits for them, and re-layouts: 0.75 us -> 5.5 us
    convert_element_type x2 -> x0, other arithmetic: 4.05 us -> none  [the longest x1 2.91 us: shards(): item_grads = gathered.reshape(rows_count, width).astype(f32)]
    pallas_call x1, Pallas kernels: 69.1 us -> 65.9 us  [shards(): pl.pallas_call(functools.partial(layer_kernel, n_dp, n_shard, capacity),...]
where the time goes in v5:
time: 73.1 us; the launch traced here: 72.1 us
  Pallas kernels  65.9 us (90%)
  local copies, waits for them, and re-layouts  5.5 us (8%)
    pallas_call x1, Pallas kernels, shards(): pl.pallas_call(functools.partial(layer_kernel, n_dp, n_shard, capacity),...  65.9 us
    unnamed x5, local copies, waits for them, and re-layouts  5.5 us

profile of v5, /device:TPU:9, one launch (start us, length us, event | category | flops | bytes accessed | tf_op | source)
XLA Modules:
  0.0 72.1 jit_solution(2689554852379843963)
XLA Ops:
  0.6 65.9 %layer.1 = (bf16[384,512]{1,0:T(8,128)(2,1)}, f32[1024,512]{1,0:T(8,128)}, f32[2,4,4,16,512]{4,3,2,1,0:T(8,128)}) custom-call(bf16[384,512]{1,0:T(8,128)(2,1)} %tokens_ref.1, bf16[512,512]{1,0:T(8,128)(2,1)} %w_ref.1, bf16[512,512]{1,0:T(8,128)(2,1)} %w_out_ref.1, bf16[1024,512]{1,0:T(8,128)(2,1)} %items_ref.1, s32[1,4]{1,0:T(1,128)} %lengths_ref.1, ...), custom_call_target="tpu_custom_call" | custom-call | tf_op jit(solution)/shard_map/layer/pallas_call | solution.py:761
  66.6 0.0 copy-start
  66.6 1.9 %copy.14 = bf16[384,512]{1,0:T(8,128)(2,1)} copy(bf16[384,512]{1,0:T(8,128)(2,1)} %get-tuple-element.12) | data formatting | bytes 786432
  68.5 2.3 %copy.15 = f32[512,512]{1,0:T(8,128)} copy(f32[512,512]{1,0:T(8,128)} %bitcast.3) | data formatting | bytes 2097152
  70.7 0.0 copy-done
  70.7 1.3 %copy.16 = f32[1024,512]{1,0:T(8,128)} copy(f32[1024,512]{1,0:T(8,128)S(1)} %copy-done) | data formatting | bytes 4194304
Async XLA Ops:
  66.6 4.2 %copy-start = (f32[1024,512]{1,0:T(8,128)S(1)}, f32[1024,512]{1,0:T(8,128)}, u32[]{:S(2)}) copy-start(f32[1024,512]{1,0:T(8,128)} %get-tuple-element.14) | copy-start | bytes 6291460

commit v6 on v5

--- a/solution.py
+++ b/solution.py
@@ -323,9 +323,8 @@
     negative_ref,
     grad_tokens_ref,
     item_grads_ref,
-    weight_grads_ref,
+    w_gathered,
     gathered,
-    w_gathered,
     w_full,
     negatives,
     requests,
@@ -720,7 +719,6 @@
     finish(height, core)
     for copy in last:
         copy.wait_recv()
-    weight_grads_ref[...] = w_gathered[...].astype(jnp.float32)
     for h in range(n_parts):
         along, pairs = shared[h]
         for k, z in enumerate(z_from):
@@ -763,13 +761,12 @@
         out_shape=[
             shape((tok_rows, width), b16),
             shape((rows_count, width), f32),
-            shape((2, n_shard, n_z, w_share, width), f32),
+            shape((2, n_shard, n_z, w_share, width), b16),
         ],
         in_specs=vmem_specs(8),
         out_specs=vmem_specs(3),
         scratch_shapes=[
             pltpu.VMEM((parts, n_z, 2, share, cols), b16),
-            pltpu.VMEM((2, n_shard, n_z, w_share, width), b16),
             pltpu.VMEM((n_shard, width, width), b16),
             pltpu.VMEM((n_shard, 2, neg_half, width), b16),
             pltpu.VMEM((n_shard, 8, capacity), jnp.int32),
@@ -821,7 +818,7 @@
         target_row,
         negative_rows.reshape(1, -1),
     )
-    return (grad_tokens, weight_grads.reshape(width, width), item_grads)
+    return (grad_tokens, weight_grads.reshape(width, width).astype(f32), item_grads)
 
 
 def fits_kernels(mesh):

time: 73.1 us -> 72.9 us (level)
  local copies, waits for them, and re-layouts: 5.5 us -> 3.09 us
  other arithmetic: 0 us -> 2.29 us
    unnamed x5 -> x4, local copies, waits for them, and re-layouts: 5.5 us -> 3.09 us
    convert_element_type x0 -> x1, other arithmetic: none -> 2.29 us  [shards(): weight_grads.reshape(width, width).astype(f32)]
where the time goes in v6:
time: 72.9 us; the launch traced here: 71.8 us
  Pallas kernels  65.8 us (90%)
  local copies, waits for them, and re-layouts  3.09 us (4%)
  other arithmetic  2.29 us (3%)
    pallas_call x1, Pallas kernels, shards(): pl.pallas_call(functools.partial(layer_kernel, n_dp, n_shard, capacity),...  65.8 us
    unnamed x4, local copies, waits for them, and re-layouts  3.09 us
    convert_element_type x1, other arithmetic, shards(): weight_grads.reshape(width, width).astype(f32)  2.29 us

profile of v6, /device:TPU:9, one launch (start us, length us, event | category | flops | bytes accessed | tf_op | source)
XLA Modules:
  0.0 71.8 jit_solution(2601148219151031446)
XLA Ops:
  0.6 65.8 %layer.1 = (bf16[384,512]{1,0:T(8,128)(2,1)}, f32[1024,512]{1,0:T(8,128)}, bf16[2,4,4,16,512]{4,3,2,1,0:T(8,128)(2,1)}) custom-call(bf16[384,512]{1,0:T(8,128)(2,1)} %tokens_ref.1, bf16[512,512]{1,0:T(8,128)(2,1)} %w_ref.1, bf16[512,512]{1,0:T(8,128)(2,1)} %w_out_ref.1, bf16[1024,512]{1,0:T(8,128)(2,1)} %items_ref.1, s32[1,4]{1,0:T(1,128)} %lengths_ref.1, ...), custom_call_target="tpu_custom_call" | custom-call | tf_op jit(solution)/shard_map/layer/pallas_call | solution.py:759
  66.4 0.0 copy-start
  66.4 2.3 %bitcast_convert_fusion = f32[512,512]{1,0:T(8,128)} fusion(bf16[2,4,4,16,512]{4,3,2,1,0:T(8,128)(2,1)} %get-tuple-element.7), kind=kLoop, calls=%fused_computation | loop fusion | flops 262144 | bytes 1572864 | tf_op jit(solution)/shard_map/convert_element_type | solution.py:821
  68.7 1.8 %copy.13 = bf16[384,512]{1,0:T(8,128)(2,1)} copy(bf16[384,512]{1,0:T(8,128)(2,1)} %get-tuple-element.12) | data formatting | bytes 786432
  70.5 0.0 copy-done
  70.5 1.3 %copy.14 = f32[1024,512]{1,0:T(8,128)} copy(f32[1024,512]{1,0:T(8,128)S(1)} %copy-done) | data formatting | bytes 4194304
Async XLA Ops:
  66.4 4.1 %copy-start = (f32[1024,512]{1,0:T(8,128)S(1)}, f32[1024,512]{1,0:T(8,128)}, u32[]{:S(2)}) copy-start(f32[1024,512]{1,0:T(8,128)} %get-tuple-element.14) | copy-start | bytes 6291460
